TPU v7x, 512 devices: a whole 4x8x8 slice. The times are simulated.
512 devices in a mesh: occ: 64 (over y, z_hi, core), vir: 8 (over x, z_lo).
Axes of the slice: x: 4, y: 8, z: 8 (z_hi: 4, z_lo: 2; z = z_hi * 2 + z_lo), core: 2. Of those that a mesh axis runs over, the one named last changes fastest.
Arguments:
- amplitudes: bfloat16 [32768, 2048], P('occ'), may hold values from -6 to 6
- integrals: bfloat16 [2048, 12288], P('occ', 'vir'), may hold values from -0.1875 to 0.1875
- row_irreps: int32 [32], replicated, may hold values from 0 to 1, as said below
- column_irreps: int32 [192], P('vir'), may hold values from 0 to 1, as said below
- occ_energy: float32 [32768], P('occ'), may hold values from -1 to -0.3
- vir_energy: float32 [12288], P('vir'), may hold values from 0.5 to 2
Outputs:
- update: bfloat16 [32768, 12288], P('occ', 'vir')
Inputs may be any that keep to these rules, and one draw needn't show every extreme that they name: `row_irreps`: each of the 2 labels is given to equally many cd tiles. `column_irreps`: each of the 2 labels is given to equally many ab tiles.
All inputs are finite; a program needn't handle non-finite values.
Results may differ from a plain program's by a relative error of at most 0.001.
Values may be sent and summed in bfloat16 or wider, within the bound.
A program may use at most 64 MiB of HBM per device.

v0:
```python
import jax
import jax.numpy as jnp
from jax import lax
from jax.sharding import PartitionSpec as P

TILE = 64


def swapped(value, axis, bit):
    mask = 2**bit
    pairs = [(source, source ^ mask) for source in range(lax.axis_size(axis))]
    return lax.ppermute(value, axis, pairs)


def body(amplitudes, integrals, row_irreps, column_irreps, occ_energy, vir_energy):
    row_labels = jnp.repeat(row_irreps, TILE)
    column_labels = jnp.repeat(column_irreps, TILE)
    top_bit = lax.axis_size("occ").bit_length() - 2
    piece = lax.all_gather(integrals, "occ", axis=0, tiled=True)
    own_ladder = jnp.dot(
        amplitudes,
        jnp.where(row_labels[:, None] == column_labels[None, :], piece, jnp.zeros_like(piece)),
        preferred_element_type=jnp.float32,
    )
    partner = swapped(own_ladder, "occ", top_bit)
    ladder = own_ladder - partner
    denominator = vir_energy[None, :] - occ_energy[:, None]
    return (ladder / denominator).astype(jnp.bfloat16)


def solution(mesh):
    placed = (P("occ", None), P("occ", "vir"), P(), P("vir"), P("occ"), P("vir"))
    return jax.shard_map(
        body, mesh=mesh, in_specs=placed, out_specs=P("occ", "vir"), check_vma=False
    )
```

profile of v0, /device:TPU:17, one launch (start us, length us, event | category | flops | bytes accessed | tf_op | source)
XLA Modules:
  0.0 272.0 jit_solution(6513135060094421712)
XLA Ops:
  6.5 0.0 copy-start
  6.5 0.0 all-gather.2.cloned.1.call-start
  6.5 0.7 all-gather.2.cloned.1.call-update
  7.3 0.7 broadcast_in_dim.12
  8.0 0.1 eq.19
  8.1 0.7 broadcast_in_dim.11
  8.8 0.1 eq.17
  8.9 0.0 copy-start.1
  8.9 0.0 copy-start.2
  8.9 101.7 %all-gather.2.cloned.1.call-done = bf16[2048,1536]{1,0:T(8,128)(2,1)} async-done(((bf16[32,1536]{1,0:T(8,128)(2,1)}), bf16[2048,1536]{1,0:T(8,128)(2,1)}) %all-gather.2.cloned.1.call-update) | async-done | bytes 6291472 | tf_op jit(solution)/shard_map/all_gather | solution.py:19
  110.6 0.0 copy-done
  110.6 6.9 %fusion.3 = f32[512,1536]{0,1:T(8,128)S(1)} fusion(bf16[512,2048]{1,0:T(8,128)(2,1)S(1)} %copy-done, bf16[2048,1536]{1,0:T(8,128)(2,1)} %all-gather.2.cloned.1.call-done, s32[1536]{0:T(1024)S(1)} %eq.19, s32[2048]{0:T(1024)S(1)} %eq.17), kind=kOutput, calls=%fused_computation.4 | convolution fusion | flops 3227516928 | bytes 11548672 | tf_op jit(solution)/shard_map/dot_general | solution.py:20
  117.5 4.0 %collective-permute-start = (f32[512,1536]{0,1:T(8,128)S(1)}, f32[512,1536]{0,1:T(8,128)S(1)}, u32[]{:S(2)}, u32[]{:S(2)}) collective-permute-start(f32[512,1536]{0,1:T(8,128)S(1)} %fusion.3), channel_id=1, source_target_pairs={{0,256},{8,264},{16,272},{24,280},{32,288},{40,296},{48,304},{56,3... | collective-permute-start | bytes 9437192 | tf_op jit(solution)/shard_map/ppermute | solution.py:12
  121.5 139.1 %collective-permute-done = f32[512,1536]{0,1:T(8,128)S(1)} collective-permute-done((f32[512,1536]{0,1:T(8,128)S(1)}, f32[512,1536]{0,1:T(8,128)S(1)}, u32[]{:S(2)}, u32[]{:S(2)}) %collective-permute-start) | collective-permute-done | bytes 3145760 | tf_op jit(solution)/shard_map/ppermute | solution.py:12
  260.6 0.0 copy-done.1
  260.6 0.0 copy-done.2
  260.6 1.9 divide_convert_fusion
  262.6 2.6 copy.7
Async XLA Ops:
  6.5 104.0 %copy-start = (bf16[512,2048]{1,0:T(8,128)(2,1)S(1)}, bf16[512,2048]{1,0:T(8,128)(2,1)}, u32[]{:S(2)}) copy-start(bf16[512,2048]{1,0:T(8,128)(2,1)} %param.6) | copy-start | bytes 6291460
  6.5 104.0 %all-gather.2.cloned.1.call-start = ((), (), s32[]{:S(2)}) async-start(), calls=%async_computation | async-start | bytes 6389760 | tf_op jit(solution)/shard_map/all_gather | solution.py:19
  8.9 251.8 %copy-start.1 = (f32[1536]{0:T(1024)S(1)}, f32[1536]{0:T(1024)}, u32[]{:S(2)}) copy-start(f32[1536]{0:T(1024)} %param.11) | copy-start | bytes 18436
  8.9 251.8 %copy-start.2 = (f32[512]{0:T(512)S(1)}, f32[512]{0:T(512)}, u32[]{:S(2)}) copy-start(f32[512]{0:T(512)} %param.10) | copy-start | bytes 6148
  117.5 143.1 %collective-permute-start = (f32[512,1536]{0,1:T(8,128)S(1)}, f32[512,1536]{0,1:T(8,128)S(1)}, u32[]{:S(2)}, u32[]{:S(2)}) collective-permute-start(f32[512,1536]{0,1:T(8,128)S(1)} %fusion.3), channel_id=1, source_target_pairs={{0,256},{8,264},{16,272},{24,280},{32,288},{40,296},{48,304},{56,3... | collective-permute-start | bytes 9437192 | tf_op jit(solution)/shard_map/ppermute | solution.py:12
Sparse Core Ops, SparseCore 0:
  10.7 99.8 all-gather.1
where the time goes:
time: 272 us
  waiting for transfers between devices  242 us (89%)
  between operations  13.4 us (5%)
  matrix products  6.9 us (3%)
  local copies, waits for them, and re-layouts  4.18 us (2%)
  starting transfers between devices  4 us (1%)
    ppermute x1, waiting for transfers between devices, swapped(): return lax.ppermute(value, axis, pairs)  139 us
    all_gather x1, waiting for transfers between devices, body(): piece = lax.all_gather(integrals, 'occ', axis=0, tiled=True)  102 us
    dot_general x1, matrix products, body(): jnp.dot(amplitudes, jnp.where(row_labels[:, None] == column_labels[None,...  6.9 us
  transfers between devices with their start and end apart: 2, of which 2 were waited for; matrix products, arithmetic and copies ran while one was open for 1% of the time, Pallas kernels for 0%

commit v1 on v0

v1 whole, which is shorter than its diff:
```python
import jax
import jax.numpy as jnp
from jax import lax
from jax.experimental import pallas as pl
from jax.experimental.pallas import tpu as pltpu
from jax.sharding import PartitionSpec as P

TILE = 64
MESH = pl.DeviceIdType.MESH
NY, NZ, NX = 8, 4, 4
Z_OFFSETS = (0, -1, 1, 2)
DELTAS = (0, 1, -1, 2, -2, 3, -3, 4)
N_SEMS = 96
ORDER = (
    ("z", 1), ("z", 2), ("relay", 1, 0), ("relay", -1, 0), ("y", 0, 1, 1), ("y", 0, 1, -1), ("zf", 0),
    ("y", 1, 1, 1), ("y", 1, 1, -1), ("own", 0), ("y", 2, 1, 1), ("y", 2, 1, -1), ("zf", -1),
    ("mir", 1, 0), ("mir", -1, 0), ("zf", 1), ("own", -1), ("y", 0, 2, 1), ("y", 0, 2, -1), ("own", 1),
    ("y", 1, 2, 1), ("y", 1, 2, -1), ("zl", 1, 0), ("x", 0, 1, 0, 1), ("x", 0, 1, 0, -1), ("y", 2, 2, 1),
    ("y", 2, 2, -1), ("zl", -1, 0), ("x", 0, -1, 0, 1), ("x", 0, -1, 0, -1), ("y", 0, 3, 1),
    ("y", 0, 3, -1), ("x", 1, 1, 0, 1), ("zf", -2), ("x", 1, 1, 0, -1), ("y", 1, 3, 1), ("y", 1, 3, -1),
    ("zf", 2), ("own", -2), ("y", 2, 3, 1), ("y", 2, 3, -1), ("xf", 0, 1, 0), ("x", 1, -1, 0, -1),
    ("y", 0, 4), ("y", 1, 4), ("own", 2), ("x", 1, -1, 0, 1), ("xf", 0, -1, 0), ("y", 2, 4), ("zf", -3),
    ("xf", 1, 1, 0), ("xf", 1, -1, 0), ("zf", 3), ("mirror", 0), ("mirror", 1), ("mirror", -1),
    ("mirror", 2), ("mirror", -2), ("zf", 4), ("full", 3), ("full", -3), ("full", 4),
)


def kernel(
    row_labels_hbm, column_labels_hbm, integrals_hbm, amplitudes, occ_energy_hbm, vir_energy_hbm, out,
    gathered, mirrored, relay, own, total, integrals, occ_energy, vir_rows, vir_energy, occ_column, row_labels, column_labels,
    send_sems, recv_sems, local_sems,
):
    occ, vir = lax.axis_index("occ"), lax.axis_index("vir")
    core = occ % 2
    zh = (occ // 2) % NZ
    y = occ // (2 * NZ)
    zl = vir % 2
    x = vir // 2

    def at(dy=0, dz=0, sibling=False):
        c = 1 - core if sibling else core
        return (((y + dy + NY) % NY) * NZ + (zh + dz + NZ) % NZ) * 2 + c

    def vir_at(dx=0, other=False):
        return ((x + dx + NX) % NX) * 2 + (1 - zl if other else zl)

    def slot(delta, stream, half=None, sibling=False):
        c = 1 - core if sibling else core
        ref = gathered.at[(y + delta + NY) % NY, (zh + Z_OFFSETS[stream] + NZ) % NZ, c]
        return ref if half is None else ref.at[pl.ds(16 * half, 16)]

    names = {}
    pending = []

    def sem_of(name):
        return names.setdefault(name, len(names))

    def send(name, source, target, to_occ=None, to_vir=None):
        k = sem_of(name)
        copy = pltpu.make_async_remote_copy(
            src_ref=source, dst_ref=target, send_sem=send_sems.at[k], recv_sem=recv_sems.at[k],
            device_id=(occ if to_occ is None else to_occ, vir if to_vir is None else to_vir),
            device_id_type=MESH,
        )
        copy.start()
        pending.append(copy)

    def arrived(name, target):
        k = sem_of(name)
        pltpu.make_async_remote_copy(
            src_ref=target, dst_ref=target, send_sem=send_sems.at[k], recv_sem=recv_sems.at[k],
            device_id=(at(sibling=True), vir), device_id_type=MESH,
        ).wait_recv()

    def half_of(distance, way):
        return None if distance < 4 else (0 if way > 0 else 1)

    def send_y(stream, distance, way):
        ref = slot(-way * (distance - 1), stream, half_of(distance, way))
        send(("y", stream, distance, way), ref, ref, to_occ=at(dy=way))

    def to_sibling(delta, stream):
        ref = slot(delta, stream)
        send(("sib", delta, stream), ref, ref, to_occ=at(sibling=True))

    def send_far(delta, stream):
        way = {1: 1, 2: -1}.get(stream)
        if way is not None:
            ref = slot(delta, stream, 0 if way > 0 else 1)
            send(("zf", delta, way), ref, ref, to_occ=at(dz=way))

    def start_stream(stream):
        send_y(stream, 1, 1)
        send_y(stream, 1, -1)
        to_sibling(0, stream)

    def on_z(stream):
        arrived(("z", stream), slot(0, stream))
        send_far(0, stream)
        start_stream(stream)

    def on_y(stream, distance, way=None):
        for w in (1, -1) if way is None else (way,):
            arrived(("y", stream, distance, w), slot(-w * distance, stream, half_of(distance, w)))
        if distance < 4:
            send_y(stream, distance + 1, way)
            send_far(-way * distance, stream)
            to_sibling(-way * distance, stream)
        else:
            send_far(4, stream)
            to_sibling(4, stream)

    def on_zf(delta):
        for way in (1, -1):
            arrived(("zf", delta, way), slot(delta, 3, 0 if way > 0 else 1))
        to_sibling(delta, 3)

    def piece(dx, other, way):
        return mirrored.at[vir_at(dx, other), 0 if way > 0 else 1]

    def on_relay(way, _):
        ref = relay.at[0 if way > 0 else 1]
        arrived(("relay", way), ref)
        send(("mir", way), ref, piece(0, False, way), to_occ=at(dy=2 * way))

    def to_x(other, way):
        ref = piece(0, other, way)
        for w in (1, -1):
            send(("x", other, way, w), ref, ref, to_vir=vir_at(w))

    def on_mir(way, _):
        ref = piece(0, False, way)
        arrived(("mir", way), ref)
        send(("zl", way), ref, ref, to_vir=vir_at(0, True))
        to_x(0, way)

    def on_zl(way, _):
        arrived(("zl", way), piece(0, True, way))
        to_x(1, way)

    def on_x(other, way, _, w):
        ref = piece(-w, other, way)
        arrived(("x", other, way, w), ref)
        if w == way:
            send(("xf", other, way), ref, ref, to_vir=vir_at(w))

    def on_xf(other, way, _):
        arrived(("xf", other, way), piece(2, other, way))

    started = []

    def chunk(delta, with_own, with_mirrored, last=False):
        first = not started
        started.append(delta)
        block = (y + delta + NY) % NY
        depth = pl.ds(pl.multiple_of(block * 256, 256), 256)

        @pl.loop(0, 6)
        def _(n):
            columns = pl.ds(pl.multiple_of(n * 256, 256), 256)
            g = gathered[block, :, :, :, columns].reshape(256, 256)
            value = None if first else total[:, columns]
            if with_own:
                term = jnp.dot(own[:, depth], g, preferred_element_type=jnp.float32)
                value = term if value is None else value + term
            if with_mirrored:
                a = mirrored[:, :, :, depth].reshape(512, 256)
                value = value - jnp.dot(a, g, preferred_element_type=jnp.float32)
            if last:
                out[:, columns] = (value / (vir_energy[n] - occ_column[...])).astype(jnp.bfloat16)
            else:
                total[:, columns] = value

    def wait_chunk(delta):
        for stream in range(4):
            arrived(("sib", delta, stream), slot(delta, stream, sibling=True))

    def on_own(delta):
        wait_chunk(delta)
        if not started:
            own_copy.wait()
        chunk(delta, True, False)

    def on_mirror(delta):
        chunk(delta, False, True)

    def on_full(delta):
        wait_chunk(delta)
        chunk(delta, True, True, last=delta == 4)

    def local(source, target, k):
        copy = pltpu.make_async_copy(source, target, local_sems.at[k])
        copy.start()
        return copy

    small = [
        local(row_labels_hbm, row_labels, 0),
        local(column_labels_hbm, column_labels, 1),
        local(integrals_hbm, integrals, 2),
        local(occ_energy_hbm, occ_energy, 3),
        local(vir_energy_hbm, vir_rows, 4),
    ]
    own_copy = local(amplitudes, own, 5)

    barrier = pltpu.get_barrier_semaphore()
    peers = [(at(dy=d), vir) for d in (1, -1, 2, -2)] + [(at(dz=d), vir) for d in (1, -1)]
    peers += [(at(sibling=True), vir), (occ, vir_at(0, True)), (occ, vir_at(1)), (occ, vir_at(-1))]
    for peer in peers:
        pl.semaphore_signal(barrier, inc=1, device_id=peer, device_id_type=MESH)

    for copy in small:
        copy.wait()
    tile_of = lax.broadcasted_iota(jnp.int32, (1, 24 * TILE), 1) // TILE
    labels = jnp.zeros((1, 24 * TILE), jnp.int32)
    for t in range(24):
        labels = jnp.where(tile_of == t, column_labels[t], labels)
    keep = jnp.broadcast_to(labels == row_labels[occ // 2], (32, 24 * TILE))
    gathered[y, zh, core] = jnp.where(keep, integrals[...].astype(jnp.float32), 0.0).astype(jnp.bfloat16)

    pl.semaphore_wait(barrier, len(peers))

    for way in (1, -1):
        half = 0 if way > 0 else 1
        rows = pl.ds(pl.multiple_of(vir * 64 + 32 * half, 32), 32)
        send(("relay", way), amplitudes.at[rows], relay.at[half], to_occ=at(dy=2 * way))
    send(("z", 1), slot(0, 0), slot(0, 0), to_occ=at(dz=1))
    send(("z", 2), slot(0, 0), slot(0, 0), to_occ=at(dz=-1))
    start_stream(0)
    for t in range(12):
        vir_energy[t // 2, :, 128 * (t % 2) : 128 * (t % 2) + 128] = vir_rows[t : t + 1, :]
    for b in range(4):
        block = jnp.transpose(jnp.broadcast_to(occ_energy[b : b + 1, :], (128, 128)))
        occ_column[128 * b : 128 * b + 128, :] = jnp.concatenate([block, block], axis=1)

    handlers = {
        "z": on_z, "y": on_y, "zf": on_zf, "relay": on_relay, "mir": on_mir, "zl": on_zl, "x": on_x, "xf": on_xf,
        "own": on_own, "mirror": on_mirror, "full": on_full,
    }
    for kind, *place in ORDER:
        handlers[kind](*place)
    for copy in pending:
        copy.wait_send()


def body(amplitudes, integrals, row_irreps, column_irreps, occ_energy, vir_energy):
    hbm = pl.BlockSpec(memory_space=pltpu.HBM)
    return pl.pallas_call(
        kernel,
        out_shape=pltpu.VMEM((512, 1536), jnp.bfloat16),
        in_specs=[hbm] * 6,
        out_specs=pl.BlockSpec(memory_space=pltpu.VMEM),
        scratch_shapes=[
            pltpu.VMEM((NY, NZ, 2, 32, 1536), jnp.bfloat16),
            pltpu.VMEM((8, 2, 32, 2048), jnp.bfloat16),
            pltpu.VMEM((2, 32, 2048), jnp.bfloat16),
            pltpu.VMEM((512, 2048), jnp.bfloat16),
            pltpu.VMEM((512, 1536), jnp.float32),
            pltpu.VMEM((32, 1536), jnp.bfloat16),
            pltpu.VMEM((4, 128), jnp.float32),
            pltpu.VMEM((12, 128), jnp.float32),
            pltpu.VMEM((6, 1, 256), jnp.float32),
            pltpu.VMEM((512, 256), jnp.float32),
            pltpu.SMEM((32,), jnp.int32),
            pltpu.SMEM((24,), jnp.int32),
            pltpu.SemaphoreType.DMA((N_SEMS,)),
            pltpu.SemaphoreType.DMA((N_SEMS,)),
            pltpu.SemaphoreType.DMA((6,)),
        ],
        compiler_params=pltpu.CompilerParams(
            collective_id=0, has_side_effects=True, vmem_limit_bytes=58 * 2**20
        ),
        cost_estimate=pl.CostEstimate(flops=6442450944, bytes_accessed=4 * 2**20, transcendentals=0),
    )(
        row_irreps, column_irreps, integrals, amplitudes,
        occ_energy.reshape(4, 128), vir_energy.reshape(12, 128),
    )


def solution(mesh):
    placed = (P("occ", None), P("occ", "vir"), P(), P("vir"), P("occ"), P("vir"))
    return jax.shard_map(
        body, mesh=mesh, in_specs=placed, out_specs=P("occ", "vir"), check_vma=False
    )
```

time: 272 us -> 70.1 us (0.26)
  the two profiles are of different devices: /device:TPU:17 before, /device:TPU:1 now
where the time goes in v1:
time: 70.1 us; the launch traced here: 69.9 us
  Pallas kernels  68.8 us (98%)
  local copies, waits for them, and re-layouts  1.15 us (2%)
    pallas_call x1, Pallas kernels, body(): pl.pallas_call(kernel, out_shape=pltpu.VMEM((512, 1536), jnp.bfloat16), i...  68.8 us

profile of v1, /device:TPU:1, one launch (start us, length us, event | category | flops | bytes accessed | tf_op | source)
XLA Modules:
  0.0 69.9 jit_solution(5143329582949629696)
XLA Ops:
  0.0 68.8 %shard_map.64 = bf16[512,1536]{1,0:T(8,128)(2,1)S(1)} custom-call(s32[32]{0:T(128)} %row_labels_hbm.1, s32[24]{0:T(128)} %column_labels_hbm.1, bf16[32,1536]{1,0:T(8,128)(2,1)} %integrals_hbm.1, bf16[512,2048]{1,0:T(8,128)(2,1)} %amplitudes.1, f32[4,128]{1,0:T(4,128)} %bitcast.3, f32[12,128]{1,0:T(8,128)} %bitcast.2), custom_call_target="tpu_custom_call" | custom-call | flops 6442450944 | bytes 4194304 | tf_op jit(solution)/shard_map/pallas_call | solution.py:247
  68.8 1.1 %copy.8 = bf16[512,1536]{1,0:T(8,128)(2,1)} copy(bf16[512,1536]{1,0:T(8,128)(2,1)S(1)} %shard_map.64) | data formatting | bytes 3145728

commit v2 on v0

v2 whole, which is shorter than its diff:
```python
import jax
import jax.numpy as jnp
from jax import lax
from jax.experimental import pallas as pl
from jax.experimental.pallas import tpu as pltpu
from jax.sharding import PartitionSpec as P

TILE = 64
MESH = pl.DeviceIdType.MESH
NY, NZ, NX = 8, 4, 4
DELTAS = (0, 1, -1, 2, -2, 3, -3, 4)
N_SEMS = 128
ORDER = (
    ("a1",), ("inverse",), ("mir", 1, 0), ("mir", -1, 0), ("a2",), ("zl", 1, 0), ("x", 0, 1, 0, 1),
    ("x", 0, 1, 0, -1), ("zl", -1, 0), ("x", 0, -1, 0, 1), ("x", 0, -1, 0, -1), ("z", 1), ("z", 3),
    ("x", 1, 1, 0, 1), ("x", 1, 1, 0, -1), ("mir", 1, 1), ("mir", -1, 1), ("xf", 0, 1, 0),
    ("x", 1, -1, 0, -1), ("y", 0, 1, 1), ("y", 0, 1, -1), ("x", 1, -1, 0, 1), ("xf", 0, -1, 0),
    ("y", 1, 1, 1), ("y", 1, 1, -1), ("zf",), ("y", 3, 1, 1), ("y", 3, 1, -1), ("xf", 1, 1, 0),
    ("x", 0, 1, 1, -1), ("zl", 1, 1), ("y", 0, 2, 1), ("y", 0, 2, -1), ("x", 0, 1, 1, 1),
    ("x", 0, -1, 1, -1), ("zl", -1, 1), ("y", 1, 2, 1), ("y", 1, 2, -1), ("x", 0, -1, 1, 1),
    ("xf", 1, -1, 0), ("y", 2, 1, 1), ("y", 2, 1, -1), ("y", 3, 2, 1), ("y", 3, 2, -1), ("x", 1, 1, 1, 1),
    ("x", 1, 1, 1, -1), ("y", 0, 3, 1), ("y", 0, 3, -1), ("unpack", 0), ("xf", 0, 1, 1), ("xf", 0, -1, 1),
    ("own", 0), ("y", 1, 3, 1), ("y", 1, 3, -1), ("x", 1, -1, 1, 1), ("x", 1, -1, 1, -1), ("y", 2, 2, 1),
    ("y", 2, 2, -1), ("y", 3, 3, 1), ("y", 3, 3, -1), ("xf", 1, 1, 1), ("y", 0, 4), ("unpack", 1),
    ("y", 1, 4), ("own", 1), ("y", 2, 3, 1), ("xf", 1, -1, 1), ("y", 2, 3, -1), ("y", 3, 4), ("mirror", 0),
    ("mirror", 1), ("y", 2, 4), ("unpack", 2), ("own", 2), ("mirror", 2), ("unpack", 3), ("own", 3),
    ("mirror", 3),
)


def kernel(
    row_labels_hbm, column_labels_hbm, integrals, amplitudes, occ_energy_hbm, vir_energy_hbm, out,
    packed_0, packed_1, packed_2, packed_3, packed_4, packed_5, packed_6, packed_7,
    first, second, mirrored, own, masked, total, inverse, occ_energy, vir_energy, occ_column, masks,
    order_vmem, order, ranks, row_labels, column_labels, send_sems, recv_sems, local_sems,
):
    packed = dict(zip(DELTAS, (packed_0, packed_1, packed_2, packed_3, packed_4, packed_5, packed_6, packed_7)))
    occ, vir = lax.axis_index("occ"), lax.axis_index("vir")
    core = occ % 2
    zh = (occ // 2) % NZ
    y = occ // (2 * NZ)
    zl = vir % 2
    x = vir // 2
    owner = zh != 3

    def at(dy=0, dz=0, sibling=False):
        c = 1 - core if sibling else core
        return (((y + dy + NY) % NY) * NZ + (zh + dz + NZ) % NZ) * 2 + c

    def vir_at(dx=0, other=False):
        return ((x + dx + NX) % NX) * 2 + (1 - zl if other else zl)

    def valid(stream):
        return (zh + stream) % NZ != 3

    names = {}
    pending = []

    def sem_of(name):
        return names.setdefault(name, len(names))

    def send(name, source, target, to_occ=None, to_vir=None, when=None):
        k = sem_of(name)

        def descriptor():
            return pltpu.make_async_remote_copy(
                src_ref=source(), dst_ref=target(), send_sem=send_sems.at[k], recv_sem=recv_sems.at[k],
                device_id=(occ if to_occ is None else to_occ, vir if to_vir is None else to_vir),
                device_id_type=MESH,
            )

        if when is None:
            descriptor().start()
            pending.append(lambda: descriptor().wait_send())
        else:
            pl.when(when)(lambda: descriptor().start())
            pending.append(lambda: pl.when(when)(lambda: descriptor().wait_send()))

    def arrived(name, target, when=None):
        k = sem_of(name)

        def wait():
            pltpu.make_async_remote_copy(
                src_ref=target(), dst_ref=target(), send_sem=send_sems.at[k], recv_sem=recv_sems.at[k],
                device_id=(at(sibling=True), vir), device_id_type=MESH,
            ).wait_recv()

        if when is None:
            wait()
        else:
            pl.when(when)(wait)

    def columns_of(t):
        return pl.ds(pl.multiple_of(512 * t, 512), 512)

    def send_first():
        for s in (1, 3, 2):
            t = (zh + s) % NZ
            send(("first", s), lambda t=t: integrals.at[:, columns_of(t)], lambda: first.at[zh], at(dz=s), when=t != 3)

    def unit(plane):
        rows = pl.ds(pl.multiple_of(16 * (plane % 2), 16), 16)
        return first.at[:, rows, pl.ds(pl.multiple_of(128 * (plane // 2), 128), 128)]

    def second_from(plane):
        return second.at[pl.ds(pl.multiple_of(4 * plane, 4), 4)]

    def on_first():
        for s in (1, 3, 2):
            arrived(("first", s), lambda s=s: first.at[(zh - s + NZ) % NZ], when=owner)

        @pl.when(owner)
        def _():
            pltpu.make_async_copy(integrals.at[:, columns_of(zh)], first.at[zh], local_sems.at[6]).wait()
            pltpu.make_async_copy(unit(y), second_from(y), local_sems.at[7]).start()

        for d in (4, 3, -3, 2, -2, 1, -1):
            plane = (y + d + NY) % NY
            send(("second", d), lambda p=plane: unit(p), lambda: second_from(y), at(dy=d), when=owner)
        for way in (1, -1):
            send_mirror(way, 1)

    def on_second():
        for d in (1, -1, 2, -2, 3, -3, 4):
            arrived(("second", d), lambda d=d: second_from((y - d + NY) % NY), when=owner)

        @pl.when(owner)
        def _():
            pltpu.make_async_copy(unit(y), second_from(y), local_sems.at[7]).wait()
            zero = masks[0, 4 * zh + y // 2].astype(jnp.float32) > 0.5

            @pl.loop(0, 16)
            def _(p):
                a = second[order[0, p]].astype(jnp.float32)
                b = second[order[0, 16 + p]].astype(jnp.float32)
                packed[0][0, core, p] = jnp.where(zero, a, b).astype(jnp.bfloat16)

        for s in (3, 1):
            send(("z", s), slot(0, 0), slot(0, s), at(dz=-s), when=owner)
        start_stream(0)

    def slot(delta, stream, half=None, sibling=False):
        def ref():
            r = packed[delta].at[stream, 1 - core if sibling else core]
            return r if half is None else r.at[pl.ds(8 * half, 8)]

        return ref

    def half_of(distance, way):
        return None if distance < 4 else (0 if way > 0 else 1)

    def delta_of(distance, way):
        return 4 if distance == 4 else -way * distance

    def send_y(stream, distance, way):
        half = half_of(distance, way)
        source = slot(delta_of(distance - 1, way), stream, half)
        target = slot(delta_of(distance, way), stream, half)
        send(("y", stream, distance, way), source, target, at(dy=way), when=valid(stream))

    def to_sibling(delta, stream):
        ref = slot(delta, stream)
        send(("sib", delta, stream), ref, ref, at(sibling=True), when=valid(stream))

    def start_stream(stream):
        send_y(stream, 1, 1)
        send_y(stream, 1, -1)
        to_sibling(0, stream)

    def on_z(stream):
        arrived(("z", stream), slot(0, stream), when=valid(stream))
        way = 1 if stream == 3 else -1
        half = 0 if way > 0 else 1
        send(("zf", half), slot(0, stream, half), slot(0, 2, half), at(dz=way), when=valid(stream))
        start_stream(stream)

    def on_zf():
        for half in (0, 1):
            arrived(("zf", half), slot(0, 2, half), when=valid(2))
        start_stream(2)

    def on_y(stream, distance, way=None):
        for w in (1, -1) if way is None else (way,):
            ref = slot(delta_of(distance, w), stream, half_of(distance, w))
            arrived(("y", stream, distance, w), ref, when=valid(stream))
        if distance < 4:
            send_y(stream, distance + 1, way)
        to_sibling(delta_of(distance, way), stream)

    def index_of(way, part):
        return part + (0 if way > 0 else 2)

    def piece(dx, other, way, part):
        return lambda: mirrored.at[vir_at(dx, other), index_of(way, part)]

    def send_mirror(way, part):
        rows = pl.ds(pl.multiple_of(vir * 64 + 16 * index_of(way, part), 16), 16)
        send(("mir", way, part), lambda: amplitudes.at[rows], piece(0, False, way, part), at(dy=4))

    def to_x(other, way, part):
        ref = piece(0, other, way, part)
        for w in (1, -1):
            send(("x", other, way, part, w), ref, ref, to_vir=vir_at(w))

    def on_mir(way, part):
        ref = piece(0, False, way, part)
        arrived(("mir", way, part), ref)
        send(("zl", way, part), ref, ref, to_vir=vir_at(0, True))
        to_x(0, way, part)

    def on_zl(way, part):
        arrived(("zl", way, part), piece(0, True, way, part))
        to_x(1, way, part)

    def on_x(other, way, part, w):
        ref = piece(-w, other, way, part)
        arrived(("x", other, way, part, w), ref)
        if w == way:
            send(("xf", other, way, part), ref, ref, to_vir=vir_at(w))

    def on_xf(other, way, part):
        arrived(("xf", other, way, part), piece(2, other, way, part))

    odd = y % 2
    groups = (
        (((0, 0), (1, 1)), ((0, -1), (1, 0)), 0, 0),
        (((0, -2), (1, -1)), ((0, 1), (1, 2)), -1, 1),
        (((0, 2), (1, 3)), ((0, -3), (1, -2)), 1, -1),
        (((0, 4), (1, -3)), ((0, 3), (1, 4)), 2, 2),
    )
    needs = ((0, 1, -1), (2, -2), (3, -3), (4,))

    def group_of(k):
        return (y // 2 + jnp.where(odd == 1, groups[k][3], groups[k][2]) + 4) % 4

    def unpack(k):
        group = group_of(k)

        def fill(planes):
            @pl.loop(0, 32)
            def _(r):
                label, rank = row_labels[r], ranks[r]
                for t in range(3):
                    keep = masks[label, 4 * t + group]
                    for parity, delta in planes:
                        for c in range(2):
                            rows = pl.ds(pl.multiple_of(r * 64 + 16 * (2 * c + parity), 16), 16)
                            value = packed[delta][(t - zh + NZ) % NZ, c, rank]
                            masked[k, rows, 128 * t : 128 * t + 128] = value * keep

        pl.when(odd == 0)(lambda: fill(groups[k][0]))
        pl.when(odd == 1)(lambda: fill(groups[k][1]))

    def own_part(k):
        return jnp.dot(own[...], masked[k], preferred_element_type=jnp.float32)

    def finish(k, value):
        group = group_of(k)
        a = mirrored[...].reshape(512, 2048)
        value = value - jnp.dot(a, masked[k], preferred_element_type=jnp.float32)
        for t in range(3):
            place = 4 * t + group
            columns = pl.ds(pl.multiple_of(128 * place, 128), 128)
            out[:, columns] = (value[:, 128 * t : 128 * t + 128] * inverse[place]).astype(jnp.bfloat16)

    def on_inverse():
        @pl.loop(0, 12)
        def _(t):
            inverse[t] = 1.0 / (vir_energy[pl.ds(t, 1), :] - occ_column[...])

    def on_unpack(k):
        for delta in needs[k]:
            for s in range(4):
                arrived(("sib", delta, s), slot(delta, s, sibling=True), when=valid(s))
        if k == 0:
            own_copy.wait()
        unpack(k)

    def on_own(k):
        total[k] = own_part(k)

    def on_mirror(k):
        finish(k, total[k])

    def local(source, target, k):
        copy = pltpu.make_async_copy(source, target, local_sems.at[k])
        copy.start()
        return copy

    labels_copies = [local(row_labels_hbm, row_labels, 0), local(column_labels_hbm, column_labels, 1)]
    energy_copies = [local(occ_energy_hbm, occ_energy, 3), local(vir_energy_hbm, vir_energy, 4)]
    own_copy = local(amplitudes, own, 5)

    @pl.when(owner)
    def _():
        pltpu.make_async_copy(integrals.at[:, columns_of(zh)], first.at[zh], local_sems.at[6]).start()

    barrier = pltpu.get_barrier_semaphore()
    peers = [(at(dy=d), vir) for d in (1, -1, 2, -2, 3, -3, 4)] + [(at(dz=d), vir) for d in (1, -1, 2)]
    peers += [(at(sibling=True), vir), (occ, vir_at(0, True)), (occ, vir_at(1)), (occ, vir_at(-1))]
    for peer in peers:
        pl.semaphore_signal(barrier, inc=1, device_id=peer, device_id_type=MESH)
    pl.semaphore_wait(barrier, len(peers))

    send_first()
    for way in (1, -1):
        send_mirror(way, 0)

    for copy in labels_copies:
        copy.wait()
    lane = lax.broadcasted_iota(jnp.int32, (8, 128), 1)
    places = jnp.zeros((8, 128), jnp.int32)
    ones = jnp.int32(0)
    for r in range(32):
        label = row_labels[r]
        rank = jnp.minimum(jnp.where(label == 1, ones, r - ones), 15)
        ranks[r] = rank
        places = jnp.where(lane == label * 16 + rank, r, places)
        ones = ones + label
    order_vmem[...] = places
    order_copy = local(order_vmem, order, 2)

    side = lax.broadcasted_iota(jnp.int32, (16, 128), 1) < TILE
    for t in range(12):
        label = jnp.where(side, column_labels[2 * t], column_labels[2 * t + 1])
        for value in (0, 1):
            masks[value, t] = jnp.where(label == value, 1.0, 0.0).astype(jnp.bfloat16)
    for copy in energy_copies:
        copy.wait()
    for b in range(4):
        occ_column[128 * b : 128 * b + 128, :] = jnp.transpose(
            jnp.broadcast_to(occ_energy[b : b + 1, :], (128, 128))
        )
    order_copy.wait()

    handlers = {
        "a1": on_first, "a2": on_second, "z": on_z, "y": on_y, "zf": on_zf, "mir": on_mir, "zl": on_zl,
        "x": on_x, "xf": on_xf, "inverse": on_inverse, "unpack": on_unpack, "own": on_own, "mirror": on_mirror,
    }
    for kind, *place in ORDER:
        handlers[kind](*place)
    for wait in pending:
        wait()


def body(amplitudes, integrals, row_irreps, column_irreps, occ_energy, vir_energy):
    hbm = pl.BlockSpec(memory_space=pltpu.HBM)
    return pl.pallas_call(
        kernel,
        out_shape=pltpu.VMEM((512, 1536), jnp.bfloat16),
        in_specs=[hbm] * 6,
        out_specs=pl.BlockSpec(memory_space=pltpu.VMEM),
        scratch_shapes=[pltpu.VMEM((4, 2, 16, 16, 128), jnp.bfloat16)] * 8
        + [
            pltpu.VMEM((4, 32, 512), jnp.bfloat16),
            pltpu.VMEM((32, 16, 128), jnp.bfloat16),
            pltpu.VMEM((8, 4, 16, 2048), jnp.bfloat16),
            pltpu.VMEM((512, 2048), jnp.bfloat16),
            pltpu.VMEM((4, 2048, 384), jnp.bfloat16),
            pltpu.VMEM((4, 512, 384), jnp.float32),
            pltpu.VMEM((12, 512, 128), jnp.float32),
            pltpu.VMEM((4, 128), jnp.float32),
            pltpu.VMEM((12, 128), jnp.float32),
            pltpu.VMEM((512, 128), jnp.float32),
            pltpu.VMEM((2, 12, 16, 128), jnp.bfloat16),
            pltpu.VMEM((8, 128), jnp.int32),
            pltpu.SMEM((8, 128), jnp.int32),
            pltpu.SMEM((32,), jnp.int32),
            pltpu.SMEM((32,), jnp.int32),
            pltpu.SMEM((24,), jnp.int32),
            pltpu.SemaphoreType.DMA((N_SEMS,)),
            pltpu.SemaphoreType.DMA((N_SEMS,)),
            pltpu.SemaphoreType.DMA((8,)),
        ],
        compiler_params=pltpu.CompilerParams(
            collective_id=0, has_side_effects=True, vmem_limit_bytes=58 * 2**20
        ),
        cost_estimate=pl.CostEstimate(flops=6442450944, bytes_accessed=4 * 2**20, transcendentals=0),
    )(
        row_irreps, column_irreps, integrals, amplitudes,
        occ_energy.reshape(4, 128), vir_energy.reshape(12, 128),
    )


def solution(mesh):
    placed = (P("occ", None), P("occ", "vir"), P(), P("vir"), P("occ"), P("vir"))
    return jax.shard_map(
        body, mesh=mesh, in_specs=placed, out_specs=P("occ", "vir"), check_vma=False
    )
```

time: 272 us -> 64.4 us (0.24)
  the two profiles are of different devices: /device:TPU:17 before, /device:TPU:1 now
where the time goes in v2:
time: 64.4 us; the launch traced here: 64.3 us
  Pallas kernels  63.2 us (98%)
  local copies, waits for them, and re-layouts  1.15 us (2%)
    pallas_call x1, Pallas kernels, body(): pl.pallas_call(kernel, out_shape=pltpu.VMEM((512, 1536), jnp.bfloat16), i...  63.2 us

profile of v2, /device:TPU:1, one launch (start us, length us, event | category | flops | bytes accessed | tf_op | source)
XLA Modules:
  0.0 64.3 jit_solution(16682275375960920066)
XLA Ops:
  0.0 63.2 %shard_map.64 = bf16[512,1536]{1,0:T(8,128)(2,1)S(1)} custom-call(s32[32]{0:T(128)} %row_labels_hbm.1, s32[24]{0:T(128)} %column_labels_hbm.1, bf16[32,1536]{1,0:T(8,128)(2,1)} %integrals.1, bf16[512,2048]{1,0:T(8,128)(2,1)} %amplitudes.1, f32[4,128]{1,0:T(4,128)} %bitcast.3, f32[12,128]{1,0:T(8,128)} %bitcast.2), custom_call_target="tpu_custom_call" | custom-call | flops 6442450944 | bytes 4194304 | tf_op jit(solution)/shard_map/pallas_call | solution.py:348
  63.2 1.1 %copy.8 = bf16[512,1536]{1,0:T(8,128)(2,1)} copy(bf16[512,1536]{1,0:T(8,128)(2,1)S(1)} %shard_map.64) | data formatting | bytes 3145728

commit v3 on v2

v3 whole, which is shorter than its diff:
```python
import jax
import jax.numpy as jnp
from jax import lax
from jax.experimental import pallas as pl
from jax.experimental.pallas import tpu as pltpu
from jax.sharding import PartitionSpec as P

TILE = 64
MESH = pl.DeviceIdType.MESH
NY, NZ, NX = 8, 4, 4
DELTAS = (0, 1, -1, 2, -2, 3, -3, 4)
N_SEMS = 128
ORDER = (
    ("sort",), ("a1",), ("inverse",), ("relay", 1, 0), ("relay", -1, 0), ("a2",), ("relay", 1, 1), ("relay", -1, 1),
    ("z", 3), ("z", 1), ("mir", 1, 0), ("mir", -1, 0), ("y", 0, 1, 1), ("y", 0, 1, -1), ("zf",),
    ("x", 0, 1, 0, 1), ("x", 0, 1, 0, -1), ("zl", 1, 0), ("mir", 1, 1), ("mir", -1, 1), ("y", 3, 1, 1),
    ("x", 0, -1, 0, 1), ("x", 0, -1, 0, -1), ("y", 3, 1, -1), ("zl", -1, 0), ("y", 1, 1, 1),
    ("y", 1, 1, -1), ("y", 0, 2, 1), ("xf", 0, 1, 0), ("y", 0, 2, -1), ("x", 1, 1, 0, -1), ("zl", 1, 1),
    ("y", 2, 1, 1), ("y", 2, 1, -1), ("x", 1, 1, 0, 1), ("x", 0, 1, 1, -1), ("zl", -1, 1), ("y", 3, 2, 1),
    ("y", 3, 2, -1), ("x", 0, 1, 1, 1), ("x", 0, -1, 1, -1), ("y", 1, 2, 1), ("y", 1, 2, -1), ("own", 0),
    ("y", 0, 3, 1), ("x", 0, -1, 1, 1), ("y", 0, 3, -1), ("xf", 0, -1, 0), ("y", 2, 2, 1), ("y", 2, 2, -1),
    ("x", 1, -1, 0, 1), ("x", 1, -1, 0, -1), ("y", 3, 3, 1), ("y", 3, 3, -1), ("x", 1, 1, 1, 1),
    ("x", 1, 1, 1, -1), ("y", 1, 3, 1), ("y", 1, 3, -1), ("own", 1), ("y", 0, 4), ("xf", 1, 1, 0),
    ("x", 1, -1, 1, -1), ("y", 2, 3, 1), ("y", 2, 3, -1), ("y", 3, 4), ("x", 1, -1, 1, 1),
    ("xf", 0, -1, 1), ("y", 1, 4), ("xf", 0, 1, 1), ("own", 2), ("xf", 1, -1, 0), ("y", 2, 4),
    ("xf", 1, 1, 1), ("xf", 1, -1, 1), ("mirror", 0), ("mirror", 1), ("mirror", 2), ("own", 3),
    ("mirror", 3),
)


def kernel(
    row_labels_hbm, column_labels_hbm, integrals, amplitudes, occ_energy_hbm, vir_energy_hbm, out,
    packed, mirrored, plain, own, total, inverse, first, second, relay, occ_energy, vir_energy, occ_column, zeros,
    order_vmem, order, row_labels, column_labels, send_sems, recv_sems, local_sems,
):
    occ, vir = lax.axis_index("occ"), lax.axis_index("vir")
    core = occ % 2
    zh = (occ // 2) % NZ
    y = occ // (2 * NZ)
    zl = vir % 2
    x = vir // 2
    owner = zh != 3

    def at(dy=0, dz=0, sibling=False):
        c = 1 - core if sibling else core
        return (((y + dy + NY) % NY) * NZ + (zh + dz + NZ) % NZ) * 2 + c

    def vir_at(dx=0, other=False):
        return ((x + dx + NX) % NX) * 2 + (1 - zl if other else zl)

    def valid(stream):
        return (zh + stream) % NZ != 3

    names = {}
    pending = []

    def sem_of(name):
        return names.setdefault(name, len(names))

    def send(name, source, target, to_occ=None, to_vir=None, when=None):
        k = sem_of(name)

        def descriptor():
            return pltpu.make_async_remote_copy(
                src_ref=source(), dst_ref=target(), send_sem=send_sems.at[k], recv_sem=recv_sems.at[k],
                device_id=(occ if to_occ is None else to_occ, vir if to_vir is None else to_vir),
                device_id_type=MESH,
            )

        if when is None:
            descriptor().start()
            pending.append(lambda: descriptor().wait_send())
        else:
            pl.when(when)(lambda: descriptor().start())
            pending.append(lambda: pl.when(when)(lambda: descriptor().wait_send()))

    def arrived(name, target, when=None):
        k = sem_of(name)

        def wait():
            pltpu.make_async_remote_copy(
                src_ref=target(), dst_ref=target(), send_sem=send_sems.at[k], recv_sem=recv_sems.at[k],
                device_id=(at(sibling=True), vir), device_id_type=MESH,
            ).wait_recv()

        if when is None:
            wait()
        else:
            pl.when(when)(wait)

    def columns_of(t):
        return pl.ds(pl.multiple_of(512 * t, 512), 512)

    def send_first():
        for s in (1, 3, 2):
            t = (zh + s) % NZ
            send(("first", s), lambda t=t: integrals.at[:, columns_of(t)], lambda: first.at[zh], at(dz=s), when=t != 3)

    def unit(plane):
        rows = pl.ds(pl.multiple_of(16 * (plane % 2), 16), 16)
        return first.at[:, rows, pl.ds(pl.multiple_of(128 * (plane // 2), 128), 128)]

    def second_from(plane):
        return second.at[pl.ds(pl.multiple_of(4 * plane, 4), 4)]

    def on_first():
        for s in (1, 3, 2):
            arrived(("first", s), lambda s=s: first.at[(zh - s + NZ) % NZ], when=owner)

        @pl.when(owner)
        def _():
            pltpu.make_async_copy(integrals.at[:, columns_of(zh)], first.at[zh], local_sems.at[6]).wait()
            pltpu.make_async_copy(unit(y), second_from(y), local_sems.at[7]).start()

        for d in (4, 3, -3, 2, -2, 1, -1):
            plane = (y + d + NY) % NY
            send(("second", d), lambda p=plane: unit(p), lambda: second_from(y), at(dy=d), when=owner)
        for way in (1, -1):
            send_mirror(way, 1)

    def on_second():
        for d in (1, -1, 2, -2, 3, -3, 4):
            arrived(("second", d), lambda d=d: second_from((y - d + NY) % NY), when=owner)

        @pl.when(owner)
        def _():
            pltpu.make_async_copy(unit(y), second_from(y), local_sems.at[7]).wait()
            zero = jnp.broadcast_to(zeros[4 * zh + y // 2], (16, 128)) == 1
            columns = pl.ds(pl.multiple_of(128 * (4 * zh + y // 2), 128), 128)

            @pl.loop(0, 16)
            def _(p):
                a = second[order[0, p]].astype(jnp.float32)
                b = second[order[0, 16 + p]].astype(jnp.float32)
                packed[p, 2 * core + y % 2, :, columns] = jnp.where(zero, a, b).astype(jnp.bfloat16)

        for s in (3, 1):
            send(("z", s), slot(0, 0), slot(0, 0), at(dz=-s), when=owner)
        start_stream(0)

    def slot(delta, stream, half=None, sibling=False):
        def ref():
            plane, block = (y + delta + NY) % NY, (zh + stream) % NZ
            rows = slice(None) if half is None else pl.ds(8 * half, 8)
            columns = pl.ds(pl.multiple_of(128 * (4 * block + plane // 2), 128), 128)
            c = 1 - core if sibling else core
            return packed.at[rows, 2 * c + plane % 2, :, columns]

        return ref

    def half_of(distance, way):
        return None if distance < 4 else (0 if way > 0 else 1)

    def delta_of(distance, way):
        return 4 if distance == 4 else -way * distance

    def send_y(stream, distance, way):
        half = half_of(distance, way)
        ref = slot(delta_of(distance - 1, way), stream, half)
        send(("y", stream, distance, way), ref, ref, at(dy=way), when=valid(stream))

    def to_sibling(delta, stream):
        ref = slot(delta, stream)
        send(("sib", delta, stream), ref, ref, at(sibling=True), when=valid(stream))

    def start_stream(stream):
        send_y(stream, 1, 1)
        send_y(stream, 1, -1)
        to_sibling(0, stream)

    def on_z(stream):
        arrived(("z", stream), slot(0, stream), when=valid(stream))
        way = 1 if stream == 3 else -1
        half = 0 if way > 0 else 1
        ref = slot(0, stream, half)
        send(("zf", half), ref, ref, at(dz=way), when=valid(stream))
        start_stream(stream)

    def on_zf():
        for half in (0, 1):
            arrived(("zf", half), slot(0, 2, half), when=valid(2))
        start_stream(2)

    def on_y(stream, distance, way=None):
        for w in (1, -1) if way is None else (way,):
            ref = slot(delta_of(distance, w), stream, half_of(distance, w))
            arrived(("y", stream, distance, w), ref, when=valid(stream))
        if distance < 4:
            send_y(stream, distance + 1, way)
        to_sibling(delta_of(distance, way), stream)

    def index_of(way, part):
        return part + (0 if way > 0 else 2)

    def piece(dx, other, way, part):
        return lambda: mirrored.at[vir_at(dx, other), index_of(way, part)]

    def relay_of(way, part):
        return lambda: relay.at[index_of(way, part)]

    def send_mirror(way, part):
        rows = pl.ds(pl.multiple_of(vir * 64 + 16 * index_of(way, part), 16), 16)
        send(("relay", way, part), lambda: own.at[rows], relay_of(way, part), at(dy=2 * way))

    def on_relay(way, part):
        arrived(("relay", way, part), relay_of(way, part))
        send(("mir", way, part), relay_of(way, part), piece(0, False, way, part), at(dy=2 * way))

    def to_x(other, way, part):
        ref = piece(0, other, way, part)
        for w in (1, -1):
            send(("x", other, way, part, w), ref, ref, to_vir=vir_at(w))

    def on_mir(way, part):
        ref = piece(0, False, way, part)
        arrived(("mir", way, part), ref)
        send(("zl", way, part), ref, ref, to_vir=vir_at(0, True))
        to_x(0, way, part)

    def on_zl(way, part):
        arrived(("zl", way, part), piece(0, True, way, part))
        to_x(1, way, part)

    def on_x(other, way, part, w):
        ref = piece(-w, other, way, part)
        arrived(("x", other, way, part, w), ref)
        if w == way:
            send(("xf", other, way, part), ref, ref, to_vir=vir_at(w))

    def on_xf(other, way, part):
        arrived(("xf", other, way, part), piece(2, other, way, part))

    odd = y % 2
    needs = ((0, 1, -1), (2, -2), (3, -3), (4,))

    def tiles_of(k):
        group = (y // 2 + jnp.where(odd == 1, (0, 1, -1, 2)[k], (0, -1, 1, 2)[k]) + 4) % 4
        return [4 * t + group for t in range(3)]

    def product(k, left):
        lanes = [pl.ds(pl.multiple_of(128 * t, 128), 128) for t in tiles_of(k)]
        right = jnp.concatenate([packed[:, :, :, n].reshape(1024, 128) for n in lanes], axis=1)
        zero = jnp.concatenate([zeros[t] for t in tiles_of(k)], axis=1) == 1
        a = jnp.dot(left(slice(0, 1024)), right, preferred_element_type=jnp.float32)
        b = jnp.dot(left(slice(1024, 2048)), right, preferred_element_type=jnp.float32)
        return jnp.where(zero, a, b)

    def on_inverse():
        @pl.loop(0, 12)
        def _(t):
            inverse[t] = 1.0 / (vir_energy[pl.ds(t, 1), :] - occ_column[...])

    def on_own(k):
        for delta in needs[k]:
            for s in range(4):
                arrived(("sib", delta, s), slot(delta, s, sibling=True), when=valid(s))
        total[k] = product(k, lambda lanes: own[:, lanes])

    def on_mirror(k):
        value = total[k] - product(k, lambda lanes: mirrored[:, :, :, lanes].reshape(512, 1024))
        for n, t in enumerate(tiles_of(k)):
            columns = pl.ds(pl.multiple_of(128 * t, 128), 128)
            out[:, columns] = (value[:, 128 * n : 128 * n + 128] * inverse[t]).astype(jnp.bfloat16)

    def sort_rows(chunk):
        rows = pl.ds(pl.multiple_of(64 * chunk, 64), 64)
        low = lax.broadcasted_iota(jnp.int32, (64, 128), 1) < TILE

        def tile(p, half):
            value = plain[order[8, p], chunk].astype(jnp.float32)
            there = jnp.broadcast_to(order[16, p], (64, 128)) == half
            return jnp.where(there, value, pltpu.roll(value, TILE, 1))

        for b in range(16):
            pair = jnp.where(low, tile(2 * b, 0), tile(2 * b + 1, 1))
            own[rows, 128 * b : 128 * b + 128] = pair.astype(jnp.bfloat16)

    def on_sort():
        @pl.loop(1, 8)
        def _(i):
            sort_rows((vir + i) % 8)

    def local(source, target, k):
        copy = pltpu.make_async_copy(source, target, local_sems.at[k])
        copy.start()
        return copy

    labels_copies = [local(row_labels_hbm, row_labels, 0), local(column_labels_hbm, column_labels, 1)]
    plain_copies = [local(amplitudes.at[:, :, pl.ds(128 * b, 128)], plain.at[b], 8 + b) for b in range(16)]
    energy_copies = [local(occ_energy_hbm, occ_energy, 3), local(vir_energy_hbm, vir_energy, 4)]

    @pl.when(owner)
    def _():
        pltpu.make_async_copy(integrals.at[:, columns_of(zh)], first.at[zh], local_sems.at[6]).start()

    barrier = pltpu.get_barrier_semaphore()
    peers = [(at(dy=d), vir) for d in (1, -1, 2, -2, 3, -3, 4)] + [(at(dz=d), vir) for d in (1, -1, 2)]
    peers += [(at(sibling=True), vir), (occ, vir_at(0, True)), (occ, vir_at(1)), (occ, vir_at(-1))]
    for peer in peers:
        pl.semaphore_signal(barrier, inc=1, device_id=peer, device_id_type=MESH)

    for copy in labels_copies:
        copy.wait()
    lane = lax.broadcasted_iota(jnp.int32, (8, 128), 1)
    places = [jnp.zeros((8, 128), jnp.int32)] * 3
    ones = jnp.int32(0)
    for r in range(32):
        label = row_labels[r]
        rank = jnp.minimum(jnp.where(label == 1, ones, r - ones), 15)
        here = lane == label * 16 + rank
        places = [jnp.where(here, n, place) for n, place in zip((r, r // 2, r % 2), places)]
        ones = ones + label
    for n in range(3):
        order_vmem[8 * n : 8 * n + 8, :] = places[n]
    order_copy = local(order_vmem, order, 2)

    pl.semaphore_wait(barrier, len(peers))
    send_first()

    for copy in plain_copies:
        copy.wait()
    order_copy.wait()
    sort_rows(vir)
    for way in (1, -1):
        send_mirror(way, 0)

    side = lax.broadcasted_iota(jnp.int32, (1, 128), 1) < TILE
    for t in range(12):
        zeros[t] = jnp.where(jnp.where(side, column_labels[2 * t], column_labels[2 * t + 1]) == 0, 1, 0)
    for copy in energy_copies:
        copy.wait()
    for b in range(4):
        occ_column[128 * b : 128 * b + 128, :] = jnp.transpose(
            jnp.broadcast_to(occ_energy[b : b + 1, :], (128, 128))
        )

    handlers = {
        "a1": on_first, "a2": on_second, "z": on_z, "y": on_y, "zf": on_zf, "relay": on_relay, "mir": on_mir,
        "zl": on_zl, "x": on_x, "xf": on_xf, "sort": on_sort, "inverse": on_inverse, "own": on_own,
        "mirror": on_mirror,
    }
    for kind, *place in ORDER:
        handlers[kind](*place)
    for wait in pending:
        wait()


def body(amplitudes, integrals, row_irreps, column_irreps, occ_energy, vir_energy):
    hbm = pl.BlockSpec(memory_space=pltpu.HBM)
    return pl.pallas_call(
        kernel,
        out_shape=pltpu.VMEM((512, 1536), jnp.bfloat16),
        in_specs=[hbm] * 6,
        out_specs=pl.BlockSpec(memory_space=pltpu.VMEM),
        scratch_shapes=[
            pltpu.VMEM((16, 4, 16, 1536), jnp.bfloat16),
            pltpu.VMEM((8, 4, 16, 2048), jnp.bfloat16),
            pltpu.VMEM((16, 8, 64, 128), jnp.bfloat16),
            pltpu.VMEM((512, 2048), jnp.bfloat16),
            pltpu.VMEM((4, 512, 384), jnp.float32),
            pltpu.VMEM((12, 512, 128), jnp.float32),
            pltpu.VMEM((4, 32, 512), jnp.bfloat16),
            pltpu.VMEM((32, 16, 128), jnp.bfloat16),
            pltpu.VMEM((4, 16, 2048), jnp.bfloat16),
            pltpu.VMEM((4, 128), jnp.float32),
            pltpu.VMEM((12, 128), jnp.float32),
            pltpu.VMEM((512, 128), jnp.float32),
            pltpu.VMEM((12, 1, 128), jnp.int32),
            pltpu.VMEM((24, 128), jnp.int32),
            pltpu.SMEM((24, 128), jnp.int32),
            pltpu.SMEM((32,), jnp.int32),
            pltpu.SMEM((24,), jnp.int32),
            pltpu.SemaphoreType.DMA((N_SEMS,)),
            pltpu.SemaphoreType.DMA((N_SEMS,)),
            pltpu.SemaphoreType.DMA((24,)),
        ],
        compiler_params=pltpu.CompilerParams(
            collective_id=0, has_side_effects=True, vmem_limit_bytes=58 * 2**20
        ),
        cost_estimate=pl.CostEstimate(flops=6442450944, bytes_accessed=4 * 2**20, transcendentals=0),
    )(
        row_irreps, column_irreps, integrals, amplitudes.reshape(8, 64, 2048),
        occ_energy.reshape(4, 128), vir_energy.reshape(12, 128),
    )


def solution(mesh):
    placed = (P("occ", None), P("occ", "vir"), P(), P("vir"), P("occ"), P("vir"))
    return jax.shard_map(
        body, mesh=mesh, in_specs=placed, out_specs=P("occ", "vir"), check_vma=False
    )
```

time: 64.4 us -> 62.3 us (0.967)
  Pallas kernels: 63.2 us -> 61 us
    pallas_call x1, Pallas kernels: 63.2 us -> 61 us  [body(): pl.pallas_call(kernel, out_shape=pltpu.VMEM((512, 1536), jnp.bfloat16), i...]
where the time goes in v3:
time: 62.3 us; the launch traced here: 62.2 us
  Pallas kernels  61 us (98%)
  local copies, waits for them, and re-layouts  1.15 us (2%)
    pallas_call x1, Pallas kernels, body(): pl.pallas_call(kernel, out_shape=pltpu.VMEM((512, 1536), jnp.bfloat16), i...  61 us

profile of v3, /device:TPU:1, one launch (start us, length us, event | category | flops | bytes accessed | tf_op | source)
XLA Modules:
  0.0 62.2 jit_solution(12438779834351104822)
XLA Ops:
  0.0 61.0 %shard_map.64 = bf16[512,1536]{1,0:T(8,128)(2,1)S(1)} custom-call(s32[32]{0:T(128)} %row_labels_hbm.1, s32[24]{0:T(128)} %column_labels_hbm.1, bf16[32,1536]{1,0:T(8,128)(2,1)} %integrals.1, bf16[8,64,2048]{2,1,0:T(8,128)(2,1)} %bitcast.3, f32[4,128]{1,0:T(4,128)} %bitcast.5, f32[12,128]{1,0:T(8,128)} %bitcast.4), custom_call_target="tpu_custom_call" | custom-call | flops 6442450944 | bytes 4194304 | tf_op jit(solution)/shard_map/pallas_call | solution.py:350
  61.0 1.1 %copy.8 = bf16[512,1536]{1,0:T(8,128)(2,1)} copy(bf16[512,1536]{1,0:T(8,128)(2,1)S(1)} %shard_map.64) | data formatting | bytes 3145728

commit v4 on v3

--- a/solution.py
+++ b/solution.py
@@ -11,28 +11,29 @@
 DELTAS = (0, 1, -1, 2, -2, 3, -3, 4)
 N_SEMS = 128
 ORDER = (
-    ("sort",), ("a1",), ("inverse",), ("relay", 1, 0), ("relay", -1, 0), ("a2",), ("relay", 1, 1), ("relay", -1, 1),
-    ("z", 3), ("z", 1), ("mir", 1, 0), ("mir", -1, 0), ("y", 0, 1, 1), ("y", 0, 1, -1), ("zf",),
-    ("x", 0, 1, 0, 1), ("x", 0, 1, 0, -1), ("zl", 1, 0), ("mir", 1, 1), ("mir", -1, 1), ("y", 3, 1, 1),
-    ("x", 0, -1, 0, 1), ("x", 0, -1, 0, -1), ("y", 3, 1, -1), ("zl", -1, 0), ("y", 1, 1, 1),
-    ("y", 1, 1, -1), ("y", 0, 2, 1), ("xf", 0, 1, 0), ("y", 0, 2, -1), ("x", 1, 1, 0, -1), ("zl", 1, 1),
-    ("y", 2, 1, 1), ("y", 2, 1, -1), ("x", 1, 1, 0, 1), ("x", 0, 1, 1, -1), ("zl", -1, 1), ("y", 3, 2, 1),
-    ("y", 3, 2, -1), ("x", 0, 1, 1, 1), ("x", 0, -1, 1, -1), ("y", 1, 2, 1), ("y", 1, 2, -1), ("own", 0),
-    ("y", 0, 3, 1), ("x", 0, -1, 1, 1), ("y", 0, 3, -1), ("xf", 0, -1, 0), ("y", 2, 2, 1), ("y", 2, 2, -1),
-    ("x", 1, -1, 0, 1), ("x", 1, -1, 0, -1), ("y", 3, 3, 1), ("y", 3, 3, -1), ("x", 1, 1, 1, 1),
-    ("x", 1, 1, 1, -1), ("y", 1, 3, 1), ("y", 1, 3, -1), ("own", 1), ("y", 0, 4), ("xf", 1, 1, 0),
-    ("x", 1, -1, 1, -1), ("y", 2, 3, 1), ("y", 2, 3, -1), ("y", 3, 4), ("x", 1, -1, 1, 1),
-    ("xf", 0, -1, 1), ("y", 1, 4), ("xf", 0, 1, 1), ("own", 2), ("xf", 1, -1, 0), ("y", 2, 4),
-    ("xf", 1, 1, 1), ("xf", 1, -1, 1), ("mirror", 0), ("mirror", 1), ("mirror", 2), ("own", 3),
+    ("a1",), ("sort",), ("relay", 1, 0), ("relay", -1, 0), ("relay", 1, 1), ("relay", -1, 1), ("a2",), ("inverse",),
+    ("mir", 1, 0), ("mir", -1, 0), ("z", 3), ("z", 1), ("mir", 1, 1), ("mir", -1, 1), ("x", 0, 1, 0, 1),
+    ("x", 0, 1, 0, -1), ("zl", 1, 0), ("y", 0, 1, 1), ("y", 0, 1, -1), ("x", 0, -1, 0, 1),
+    ("x", 0, -1, 0, -1), ("zl", -1, 0), ("y", 3, 1, 1), ("y", 3, 1, -1), ("zf",), ("y", 1, 1, 1),
+    ("y", 1, 1, -1), ("x", 0, 1, 1, 1), ("x", 0, 1, 1, -1), ("y", 0, 2, 1), ("y", 0, 2, -1), ("zl", 1, 1),
+    ("x", 0, -1, 1, 1), ("x", 0, -1, 1, -1), ("y", 3, 2, 1), ("y", 3, 2, -1), ("zl", -1, 1),
+    ("xf", 0, 1, 0), ("xf", 0, -1, 0), ("y", 2, 1, 1), ("y", 2, 1, -1), ("x", 1, 1, 0, 1), ("y", 1, 2, 1),
+    ("y", 1, 2, -1), ("xf", 0, 1, 1), ("x", 1, 1, 1, -1), ("y", 0, 3, 1), ("y", 0, 3, -1), ("own", 0),
+    ("x", 1, 1, 0, -1), ("x", 1, 1, 1, 1), ("y", 3, 3, 1), ("xf", 0, -1, 1), ("y", 3, 3, -1),
+    ("x", 1, -1, 0, 1), ("x", 1, -1, 1, 1), ("y", 2, 2, 1), ("y", 2, 2, -1), ("x", 1, -1, 1, -1),
+    ("x", 1, -1, 0, -1), ("y", 1, 3, 1), ("y", 1, 3, -1), ("y", 0, 4), ("y", 3, 4), ("own", 1),
+    ("xf", 1, 1, 0), ("xf", 1, 1, 1), ("y", 2, 3, 1), ("y", 2, 3, -1), ("y", 1, 4), ("xf", 1, -1, 0),
+    ("xf", 1, -1, 1), ("mirror", 0), ("mirror", 1), ("y", 2, 4), ("own", 2), ("mirror", 2), ("own", 3),
     ("mirror", 3),
 )
 
 
 def kernel(
     row_labels_hbm, column_labels_hbm, integrals, amplitudes, occ_energy_hbm, vir_energy_hbm, out,
-    packed, mirrored, plain, own, total, inverse, first, second, relay, occ_energy, vir_energy, occ_column, zeros,
+    packed, mirrored, plain, own, total, inverse, first, second, relay, landed_0, landed_1, landed_2, landed_3, occ_energy, vir_energy, occ_column, zeros,
     order_vmem, order, row_labels, column_labels, send_sems, recv_sems, local_sems,
 ):
+    landed = (landed_0, landed_1, landed_2, landed_3)
     occ, vir = lax.axis_index("occ"), lax.axis_index("vir")
     core = occ % 2
     zh = (occ // 2) % NZ
@@ -115,8 +116,6 @@
         for d in (4, 3, -3, 2, -2, 1, -1):
             plane = (y + d + NY) % NY
             send(("second", d), lambda p=plane: unit(p), lambda: second_from(y), at(dy=d), when=owner)
-        for way in (1, -1):
-            send_mirror(way, 1)
 
     def on_second():
         for d in (1, -1, 2, -2, 3, -3, 4):
@@ -198,37 +197,58 @@
     def relay_of(way, part):
         return lambda: relay.at[index_of(way, part)]
 
+    def landed_of(way, part):
+        return lambda: landed[index_of(way, part)]
+
     def send_mirror(way, part):
-        rows = pl.ds(pl.multiple_of(vir * 64 + 16 * index_of(way, part), 16), 16)
-        send(("relay", way, part), lambda: own.at[rows], relay_of(way, part), at(dy=2 * way))
+        rows = pl.ds(16 * index_of(way, part), 16)
+        send(("relay", way, part), lambda: plain.at[:, vir, rows], relay_of(way, part), at(dy=2 * way))
 
     def on_relay(way, part):
         arrived(("relay", way, part), relay_of(way, part))
-        send(("mir", way, part), relay_of(way, part), piece(0, False, way, part), at(dy=2 * way))
+        send(("mir", way, part), relay_of(way, part), landed_of(way, part), at(dy=2 * way))
 
     def to_x(other, way, part):
         ref = piece(0, other, way, part)
         for w in (1, -1):
             send(("x", other, way, part, w), ref, ref, to_vir=vir_at(w))
 
+    def to_other(name, ref):
+        send(name, ref, ref, to_vir=vir_at(0, True))
+
     def on_mir(way, part):
-        ref = piece(0, False, way, part)
-        arrived(("mir", way, part), ref)
-        send(("zl", way, part), ref, ref, to_vir=vir_at(0, True))
-        to_x(0, way, part)
+        arrived(("mir", way, part), landed_of(way, part))
+        n = index_of(way, part)
+        for b in range(16):
+            mirrored[vir, n, :, 128 * b : 128 * b + 128] = sorted_block(lambda i: landed[n][i], b, 16)
+        if part == 0:
+            to_x(0, way, part)
+            to_other(("zl", way, part), piece(0, False, way, part))
+        else:
+            to_other(("zl", way, part), piece(0, False, way, part))
+            to_x(0, way, part)
 
     def on_zl(way, part):
         arrived(("zl", way, part), piece(0, True, way, part))
-        to_x(1, way, part)
+        if part == 1:
+            to_x(1, way, part)
 
     def on_x(other, way, part, w):
+        if other and part == 0:
+            arrived(("x", 1, way, part, w), piece(-w, True, way, part))
+            return
         ref = piece(-w, other, way, part)
         arrived(("x", other, way, part, w), ref)
         if w == way:
             send(("xf", other, way, part), ref, ref, to_vir=vir_at(w))
+        if part == 0:
+            to_other(("x", 1, way, part, w), ref)
 
     def on_xf(other, way, part):
-        arrived(("xf", other, way, part), piece(2, other, way, part))
+        ref = piece(2, other, way, part)
+        arrived(("xf", other, way, part), ref)
+        if part == 0 and not other:
+            to_other(("xf", 1, way, part), ref)
 
     odd = y % 2
     needs = ((0, 1, -1), (2, -2), (3, -3), (4,))
@@ -262,23 +282,22 @@
             columns = pl.ds(pl.multiple_of(128 * t, 128), 128)
             out[:, columns] = (value[:, 128 * n : 128 * n + 128] * inverse[t]).astype(jnp.bfloat16)
 
-    def sort_rows(chunk):
-        rows = pl.ds(pl.multiple_of(64 * chunk, 64), 64)
-        low = lax.broadcasted_iota(jnp.int32, (64, 128), 1) < TILE
+    def sorted_block(block, b, rows):
+        low = lax.broadcasted_iota(jnp.int32, (rows, 128), 1) < TILE
 
         def tile(p, half):
-            value = plain[order[8, p], chunk].astype(jnp.float32)
-            there = jnp.broadcast_to(order[16, p], (64, 128)) == half
+            value = block(order[8, p]).astype(jnp.float32)
+            there = jnp.broadcast_to(order[16, p], (rows, 128)) == half
             return jnp.where(there, value, pltpu.roll(value, TILE, 1))
 
-        for b in range(16):
-            pair = jnp.where(low, tile(2 * b, 0), tile(2 * b + 1, 1))
-            own[rows, 128 * b : 128 * b + 128] = pair.astype(jnp.bfloat16)
+        return jnp.where(low, tile(2 * b, 0), tile(2 * b + 1, 1)).astype(jnp.bfloat16)
 
     def on_sort():
-        @pl.loop(1, 8)
-        def _(i):
-            sort_rows((vir + i) % 8)
+        @pl.loop(0, 8)
+        def _(chunk):
+            rows = pl.ds(pl.multiple_of(64 * chunk, 64), 64)
+            for b in range(16):
+                own[rows, 128 * b : 128 * b + 128] = sorted_block(lambda i: plain[i, chunk], b, 64)
 
     def local(source, target, k):
         copy = pltpu.make_async_copy(source, target, local_sems.at[k])
@@ -298,6 +317,14 @@
     peers += [(at(sibling=True), vir), (occ, vir_at(0, True)), (occ, vir_at(1)), (occ, vir_at(-1))]
     for peer in peers:
         pl.semaphore_signal(barrier, inc=1, device_id=peer, device_id_type=MESH)
+
+    pl.semaphore_wait(barrier, len(peers))
+    send_first()
+    for copy in plain_copies:
+        copy.wait()
+    for part in (0, 1):
+        for way in (1, -1):
+            send_mirror(way, part)
 
     for copy in labels_copies:
         copy.wait()
@@ -314,16 +341,6 @@
         order_vmem[8 * n : 8 * n + 8, :] = places[n]
     order_copy = local(order_vmem, order, 2)
 
-    pl.semaphore_wait(barrier, len(peers))
-    send_first()
-
-    for copy in plain_copies:
-        copy.wait()
-    order_copy.wait()
-    sort_rows(vir)
-    for way in (1, -1):
-        send_mirror(way, 0)
-
     side = lax.broadcasted_iota(jnp.int32, (1, 128), 1) < TILE
     for t in range(12):
         zeros[t] = jnp.where(jnp.where(side, column_labels[2 * t], column_labels[2 * t + 1]) == 0, 1, 0)
@@ -333,6 +350,7 @@
         occ_column[128 * b : 128 * b + 128, :] = jnp.transpose(
             jnp.broadcast_to(occ_energy[b : b + 1, :], (128, 128))
         )
+    order_copy.wait()
 
     handlers = {
         "a1": on_first, "a2": on_second, "z": on_z, "y": on_y, "zf": on_zf, "relay": on_relay, "mir": on_mir,
@@ -361,7 +379,8 @@
             pltpu.VMEM((12, 512, 128), jnp.float32),
             pltpu.VMEM((4, 32, 512), jnp.bfloat16),
             pltpu.VMEM((32, 16, 128), jnp.bfloat16),
-            pltpu.VMEM((4, 16, 2048), jnp.bfloat16),
+            pltpu.VMEM((4, 16, 16, 128), jnp.bfloat16),
+            *[pltpu.VMEM((16, 16, 128), jnp.bfloat16)] * 4,
             pltpu.VMEM((4, 128), jnp.float32),
             pltpu.VMEM((12, 128), jnp.float32),
             pltpu.VMEM((512, 128), jnp.float32),

time: 62.3 us -> 59.4 us (0.953)
  Pallas kernels: 61 us -> 58.1 us
    pallas_call x1, Pallas kernels: 61 us -> 58.1 us  [body(): pl.pallas_call(kernel, out_shape=pltpu.VMEM((512, 1536), jnp.bfloat16), i...]
where the time goes in v4:
time: 59.4 us; the launch traced here: 59.3 us
  Pallas kernels  58.1 us (98%)
  local copies, waits for them, and re-layouts  1.15 us (2%)
    pallas_call x1, Pallas kernels, body(): pl.pallas_call(kernel, out_shape=pltpu.VMEM((512, 1536), jnp.bfloat16), i...  58.1 us

profile of v4, /device:TPU:1, one launch (start us, length us, event | category | flops | bytes accessed | tf_op | source)
XLA Modules:
  0.0 59.3 jit_solution(1602295805524825882)
XLA Ops:
  0.0 58.1 %shard_map.64 = bf16[512,1536]{1,0:T(8,128)(2,1)S(1)} custom-call(s32[32]{0:T(128)} %row_labels_hbm.1, s32[24]{0:T(128)} %column_labels_hbm.1, bf16[32,1536]{1,0:T(8,128)(2,1)} %integrals.1, bf16[8,64,2048]{2,1,0:T(8,128)(2,1)} %bitcast.3, f32[4,128]{1,0:T(4,128)} %bitcast.5, f32[12,128]{1,0:T(8,128)} %bitcast.4), custom_call_target="tpu_custom_call" | custom-call | flops 6442450944 | bytes 4194304 | tf_op jit(solution)/shard_map/pallas_call | solution.py:368
  58.1 1.1 %copy.8 = bf16[512,1536]{1,0:T(8,128)(2,1)} copy(bf16[512,1536]{1,0:T(8,128)(2,1)S(1)} %shard_map.64) | data formatting | bytes 3145728

commit v5 on v4

--- a/solution.py
+++ b/solution.py
@@ -11,20 +11,21 @@
 DELTAS = (0, 1, -1, 2, -2, 3, -3, 4)
 N_SEMS = 128
 ORDER = (
-    ("a1",), ("sort",), ("relay", 1, 0), ("relay", -1, 0), ("relay", 1, 1), ("relay", -1, 1), ("a2",), ("inverse",),
-    ("mir", 1, 0), ("mir", -1, 0), ("z", 3), ("z", 1), ("mir", 1, 1), ("mir", -1, 1), ("x", 0, 1, 0, 1),
-    ("x", 0, 1, 0, -1), ("zl", 1, 0), ("y", 0, 1, 1), ("y", 0, 1, -1), ("x", 0, -1, 0, 1),
-    ("x", 0, -1, 0, -1), ("zl", -1, 0), ("y", 3, 1, 1), ("y", 3, 1, -1), ("zf",), ("y", 1, 1, 1),
-    ("y", 1, 1, -1), ("x", 0, 1, 1, 1), ("x", 0, 1, 1, -1), ("y", 0, 2, 1), ("y", 0, 2, -1), ("zl", 1, 1),
-    ("x", 0, -1, 1, 1), ("x", 0, -1, 1, -1), ("y", 3, 2, 1), ("y", 3, 2, -1), ("zl", -1, 1),
-    ("xf", 0, 1, 0), ("xf", 0, -1, 0), ("y", 2, 1, 1), ("y", 2, 1, -1), ("x", 1, 1, 0, 1), ("y", 1, 2, 1),
-    ("y", 1, 2, -1), ("xf", 0, 1, 1), ("x", 1, 1, 1, -1), ("y", 0, 3, 1), ("y", 0, 3, -1), ("own", 0),
-    ("x", 1, 1, 0, -1), ("x", 1, 1, 1, 1), ("y", 3, 3, 1), ("xf", 0, -1, 1), ("y", 3, 3, -1),
-    ("x", 1, -1, 0, 1), ("x", 1, -1, 1, 1), ("y", 2, 2, 1), ("y", 2, 2, -1), ("x", 1, -1, 1, -1),
-    ("x", 1, -1, 0, -1), ("y", 1, 3, 1), ("y", 1, 3, -1), ("y", 0, 4), ("y", 3, 4), ("own", 1),
-    ("xf", 1, 1, 0), ("xf", 1, 1, 1), ("y", 2, 3, 1), ("y", 2, 3, -1), ("y", 1, 4), ("xf", 1, -1, 0),
-    ("xf", 1, -1, 1), ("mirror", 0), ("mirror", 1), ("y", 2, 4), ("own", 2), ("mirror", 2), ("own", 3),
-    ("mirror", 3),
+    ("a1",), ("sort",), ("relay", 1, 0), ("relay", 1, 1), ("relay", -1, 0), ("relay", -1, 1), ("a2",), ("inverse",),
+    ("mir", 1, 0), ("mir", -1, 0), ("z", 3), ("mir", 1, 1), ("z", 1), ("mir", -1, 1), ("y", 0, 1, 1),
+    ("y", 0, 1, -1), ("z", 2), ("x", 0, -1, 0, -1), ("y", 3, 1, -1), ("x", 0, 1, 0, 1), ("x", 0, -1, 0, 1),
+    ("y", 3, 1, 1), ("y", 1, 1, 1), ("y", 1, 1, -1), ("y", 0, 2, 1), ("y", 0, 2, -1), ("x", 0, 1, 0, -1),
+    ("zl", 1, 1), ("y", 2, 1, 1), ("zl", -1, 0), ("y", 2, 1, -1), ("x", 0, -1, 1, 1), ("zl", -1, 1),
+    ("zl", 1, 0), ("x", 0, 1, 1, -1), ("xf", 0, -1, 0), ("x", 0, -1, 1, -1), ("y", 3, 2, 1),
+    ("y", 3, 2, -1), ("xf", 0, 1, 0), ("y", 1, 2, -1), ("y", 1, 2, 1), ("y", 0, 3, 1), ("y", 0, 3, -1),
+    ("own", 0, 0), ("y", 2, 2, 1), ("x", 1, 1, 1, -1), ("y", 2, 2, -1), ("x", 1, 1, 1, 1), ("own", 3, 0),
+    ("y", 3, 3, -1), ("y", 3, 3, 1), ("x", 0, 1, 1, 1), ("x", 1, -1, 1, -1), ("y", 1, 3, 1),
+    ("y", 1, 3, -1), ("y", 0, 4), ("x", 1, -1, 0, -1), ("own", 1, 0), ("y", 2, 3, -1), ("y", 2, 3, 1),
+    ("x", 1, -1, 1, 1), ("x", 1, 1, 0, 1), ("y", 3, 4), ("xf", 1, -1, 0), ("xf", 0, -1, 1), ("own", 2, 0),
+    ("y", 1, 4), ("own", 0, 1), ("xf", 1, -1, 1), ("xf", 0, 1, 1), ("x", 1, -1, 0, 1), ("x", 1, 1, 0, -1),
+    ("xf", 1, 1, 0), ("xf", 1, 1, 1), ("mirror", 0, 1), ("mirror", 1, 0), ("mirror", 0, 0), ("y", 2, 4),
+    ("mirror", 3, 0), ("own", 3, 1), ("own", 1, 1), ("mirror", 3, 1), ("mirror", 1, 1), ("mirror", 2, 0),
+    ("own", 2, 1), ("mirror", 2, 1),
 )
 
 
@@ -136,6 +137,7 @@
         for s in (3, 1):
             send(("z", s), slot(0, 0), slot(0, 0), at(dz=-s), when=owner)
         start_stream(0)
+        send(("z", 2), slot(0, 0), slot(0, 0), at(dz=2), when=owner)
 
     def slot(delta, stream, half=None, sibling=False):
         def ref():
@@ -169,16 +171,7 @@
 
     def on_z(stream):
         arrived(("z", stream), slot(0, stream), when=valid(stream))
-        way = 1 if stream == 3 else -1
-        half = 0 if way > 0 else 1
-        ref = slot(0, stream, half)
-        send(("zf", half), ref, ref, at(dz=way), when=valid(stream))
         start_stream(stream)
-
-    def on_zf():
-        for half in (0, 1):
-            arrived(("zf", half), slot(0, 2, half), when=valid(2))
-        start_stream(2)
 
     def on_y(stream, distance, way=None):
         for w in (1, -1) if way is None else (way,):
@@ -219,8 +212,12 @@
     def on_mir(way, part):
         arrived(("mir", way, part), landed_of(way, part))
         n = index_of(way, part)
-        for b in range(16):
-            mirrored[vir, n, :, 128 * b : 128 * b + 128] = sorted_block(lambda i: landed[n][i], b, 16)
+
+        @pl.loop(0, 16, unroll=8)
+        def _(b):
+            lanes = pl.ds(pl.multiple_of(128 * b, 128), 128)
+            mirrored[vir, n, :, lanes] = sorted_block(lambda i: landed[n][i], b, 16)
+
         if part == 0:
             to_x(0, way, part)
             to_other(("zl", way, part), piece(0, False, way, part))
@@ -251,16 +248,17 @@
             to_other(("xf", 1, way, part), ref)
 
     odd = y % 2
-    needs = ((0, 1, -1), (2, -2), (3, -3), (4,))
-
-    def tiles_of(k):
-        group = (y // 2 + jnp.where(odd == 1, (0, 1, -1, 2)[k], (0, -1, 1, 2)[k]) + 4) % 4
-        return [4 * t + group for t in range(3)]
-
-    def product(k, left):
-        lanes = [pl.ds(pl.multiple_of(128 * t, 128), 128) for t in tiles_of(k)]
+    needs = ((0, 1, -1, 2, -2), (3, -3, 4))
+
+    def tiles_of(stream, half):
+        steps = (((0, 0), (-1, 1)), ((1, -1), (2, 2)))[half]
+        block = (zh + stream) % NZ
+        return [4 * block + (y // 2 + jnp.where(odd == 1, o, e) + 4) % 4 for e, o in steps]
+
+    def product(tiles, left):
+        lanes = [pl.ds(pl.multiple_of(128 * t, 128), 128) for t in tiles]
         right = jnp.concatenate([packed[:, :, :, n].reshape(1024, 128) for n in lanes], axis=1)
-        zero = jnp.concatenate([zeros[t] for t in tiles_of(k)], axis=1) == 1
+        zero = jnp.concatenate([zeros[t] for t in tiles], axis=1) == 1
         a = jnp.dot(left(slice(0, 1024)), right, preferred_element_type=jnp.float32)
         b = jnp.dot(left(slice(1024, 2048)), right, preferred_element_type=jnp.float32)
         return jnp.where(zero, a, b)
@@ -270,17 +268,23 @@
         def _(t):
             inverse[t] = 1.0 / (vir_energy[pl.ds(t, 1), :] - occ_column[...])
 
-    def on_own(k):
-        for delta in needs[k]:
-            for s in range(4):
-                arrived(("sib", delta, s), slot(delta, s, sibling=True), when=valid(s))
-        total[k] = product(k, lambda lanes: own[:, lanes])
-
-    def on_mirror(k):
-        value = total[k] - product(k, lambda lanes: mirrored[:, :, :, lanes].reshape(512, 1024))
-        for n, t in enumerate(tiles_of(k)):
-            columns = pl.ds(pl.multiple_of(128 * t, 128), 128)
-            out[:, columns] = (value[:, 128 * n : 128 * n + 128] * inverse[t]).astype(jnp.bfloat16)
+    def on_own(stream, half):
+        @pl.when(valid(stream))
+        def _():
+            for delta in needs[half]:
+                arrived(("sib", delta, stream), slot(delta, stream, sibling=True))
+            total[2 * stream + half] = product(tiles_of(stream, half), lambda lanes: own[:, lanes])
+
+    def on_mirror(stream, half):
+        @pl.when(valid(stream))
+        def _():
+            tiles = tiles_of(stream, half)
+            value = total[2 * stream + half] - product(
+                tiles, lambda lanes: mirrored[:, :, :, lanes].reshape(512, 1024)
+            )
+            for n, t in enumerate(tiles):
+                columns = pl.ds(pl.multiple_of(128 * t, 128), 128)
+                out[:, columns] = (value[:, 128 * n : 128 * n + 128] * inverse[t]).astype(jnp.bfloat16)
 
     def sorted_block(block, b, rows):
         low = lax.broadcasted_iota(jnp.int32, (rows, 128), 1) < TILE
@@ -293,11 +297,10 @@
         return jnp.where(low, tile(2 * b, 0), tile(2 * b + 1, 1)).astype(jnp.bfloat16)
 
     def on_sort():
-        @pl.loop(0, 8)
-        def _(chunk):
-            rows = pl.ds(pl.multiple_of(64 * chunk, 64), 64)
-            for b in range(16):
-                own[rows, 128 * b : 128 * b + 128] = sorted_block(lambda i: plain[i, chunk], b, 64)
+        @pl.loop(0, 16)
+        def _(b):
+            lanes = pl.ds(pl.multiple_of(128 * b, 128), 128)
+            own[:, lanes] = sorted_block(lambda i: plain[i].reshape(512, 128), b, 512)
 
     def local(source, target, k):
         copy = pltpu.make_async_copy(source, target, local_sems.at[k])
@@ -353,7 +356,7 @@
     order_copy.wait()
 
     handlers = {
-        "a1": on_first, "a2": on_second, "z": on_z, "y": on_y, "zf": on_zf, "relay": on_relay, "mir": on_mir,
+        "a1": on_first, "a2": on_second, "z": on_z, "y": on_y, "relay": on_relay, "mir": on_mir,
         "zl": on_zl, "x": on_x, "xf": on_xf, "sort": on_sort, "inverse": on_inverse, "own": on_own,
         "mirror": on_mirror,
     }
@@ -375,7 +378,7 @@
             pltpu.VMEM((8, 4, 16, 2048), jnp.bfloat16),
             pltpu.VMEM((16, 8, 64, 128), jnp.bfloat16),
             pltpu.VMEM((512, 2048), jnp.bfloat16),
-            pltpu.VMEM((4, 512, 384), jnp.float32),
+            pltpu.VMEM((8, 512, 256), jnp.float32),
             pltpu.VMEM((12, 512, 128), jnp.float32),
             pltpu.VMEM((4, 32, 512), jnp.bfloat16),
             pltpu.VMEM((32, 16, 128), jnp.bfloat16),

time: 59.4 us -> 57.6 us (0.970)
  Pallas kernels: 58.1 us -> 56.4 us
    pallas_call x1, Pallas kernels: 58.1 us -> 56.4 us  [body(): pl.pallas_call(kernel, out_shape=pltpu.VMEM((512, 1536), jnp.bfloat16), i...]
where the time goes in v5:
time: 57.6 us; the launch traced here: 57.5 us
  Pallas kernels  56.4 us (98%)
  local copies, waits for them, and re-layouts  1.15 us (2%)
    pallas_call x1, Pallas kernels, body(): pl.pallas_call(kernel, out_shape=pltpu.VMEM((512, 1536), jnp.bfloat16), i...  56.4 us

profile of v5, /device:TPU:1, one launch (start us, length us, event | category | flops | bytes accessed | tf_op | source)
XLA Modules:
  0.0 57.5 jit_solution(17806932820741366441)
XLA Ops:
  0.0 56.4 %shard_map.64 = bf16[512,1536]{1,0:T(8,128)(2,1)S(1)} custom-call(s32[32]{0:T(128)} %row_labels_hbm.1, s32[24]{0:T(128)} %column_labels_hbm.1, bf16[32,1536]{1,0:T(8,128)(2,1)} %integrals.1, bf16[8,64,2048]{2,1,0:T(8,128)(2,1)} %bitcast.3, f32[4,128]{1,0:T(4,128)} %bitcast.5, f32[12,128]{1,0:T(8,128)} %bitcast.4), custom_call_target="tpu_custom_call" | custom-call | flops 6442450944 | bytes 4194304 | tf_op jit(solution)/shard_map/pallas_call | solution.py:371
  56.4 1.1 %copy.8 = bf16[512,1536]{1,0:T(8,128)(2,1)} copy(bf16[512,1536]{1,0:T(8,128)(2,1)S(1)} %shard_map.64) | data formatting | bytes 3145728

commit v6 on v5

--- a/solution.py
+++ b/solution.py
@@ -11,21 +11,24 @@
 DELTAS = (0, 1, -1, 2, -2, 3, -3, 4)
 N_SEMS = 128
 ORDER = (
-    ("a1",), ("sort",), ("relay", 1, 0), ("relay", 1, 1), ("relay", -1, 0), ("relay", -1, 1), ("a2",), ("inverse",),
-    ("mir", 1, 0), ("mir", -1, 0), ("z", 3), ("mir", 1, 1), ("z", 1), ("mir", -1, 1), ("y", 0, 1, 1),
-    ("y", 0, 1, -1), ("z", 2), ("x", 0, -1, 0, -1), ("y", 3, 1, -1), ("x", 0, 1, 0, 1), ("x", 0, -1, 0, 1),
-    ("y", 3, 1, 1), ("y", 1, 1, 1), ("y", 1, 1, -1), ("y", 0, 2, 1), ("y", 0, 2, -1), ("x", 0, 1, 0, -1),
-    ("zl", 1, 1), ("y", 2, 1, 1), ("zl", -1, 0), ("y", 2, 1, -1), ("x", 0, -1, 1, 1), ("zl", -1, 1),
-    ("zl", 1, 0), ("x", 0, 1, 1, -1), ("xf", 0, -1, 0), ("x", 0, -1, 1, -1), ("y", 3, 2, 1),
-    ("y", 3, 2, -1), ("xf", 0, 1, 0), ("y", 1, 2, -1), ("y", 1, 2, 1), ("y", 0, 3, 1), ("y", 0, 3, -1),
-    ("own", 0, 0), ("y", 2, 2, 1), ("x", 1, 1, 1, -1), ("y", 2, 2, -1), ("x", 1, 1, 1, 1), ("own", 3, 0),
-    ("y", 3, 3, -1), ("y", 3, 3, 1), ("x", 0, 1, 1, 1), ("x", 1, -1, 1, -1), ("y", 1, 3, 1),
-    ("y", 1, 3, -1), ("y", 0, 4), ("x", 1, -1, 0, -1), ("own", 1, 0), ("y", 2, 3, -1), ("y", 2, 3, 1),
-    ("x", 1, -1, 1, 1), ("x", 1, 1, 0, 1), ("y", 3, 4), ("xf", 1, -1, 0), ("xf", 0, -1, 1), ("own", 2, 0),
-    ("y", 1, 4), ("own", 0, 1), ("xf", 1, -1, 1), ("xf", 0, 1, 1), ("x", 1, -1, 0, 1), ("x", 1, 1, 0, -1),
-    ("xf", 1, 1, 0), ("xf", 1, 1, 1), ("mirror", 0, 1), ("mirror", 1, 0), ("mirror", 0, 0), ("y", 2, 4),
-    ("mirror", 3, 0), ("own", 3, 1), ("own", 1, 1), ("mirror", 3, 1), ("mirror", 1, 1), ("mirror", 2, 0),
-    ("own", 2, 1), ("mirror", 2, 1),
+    ("sort", 4), ("sort", 7), ("sort", 6), ("sort", 1), ("sort", 0), ("a1",), ("inverse", 3), ("relay", 1, 0),
+    ("relay", -1, 0), ("relay", 1, 1), ("a2",), ("relay", -1, 1), ("mir", 1, 0),
+    ("inverse", 1), ("inverse", 2), ("mir", -1, 0), ("sort", 3), ("z", 3), ("mir", 1, 1), ("z", 1),
+    ("y", 0, 1, -1), ("flush", 30), ("y", 0, 1, 1), ("mir", -1, 1), ("x", 0, 1, 0, -1), ("z", 2),
+    ("flush", 30), ("y", 3, 1, -1), ("x", 0, -1, 0, -1), ("y", 3, 1, 1), ("sort", 2), ("flush", 30),
+    ("y", 1, 1, -1), ("y", 1, 1, 1), ("zl", -1, 0), ("x", 0, 1, 0, 1), ("y", 0, 2, 1), ("y", 0, 2, -1),
+    ("zl", 1, 0), ("flush", 30), ("zl", 1, 1), ("x", 0, 1, 1, 1), ("inverse", 0), ("x", 0, -1, 1, 1),
+    ("y", 2, 1, -1), ("y", 2, 1, 1), ("flush", 30), ("y", 3, 2, 1), ("zl", -1, 1), ("x", 0, 1, 1, -1),
+    ("x", 0, -1, 1, -1), ("y", 3, 2, -1), ("flush", 30), ("y", 1, 2, -1), ("xf", 0, 1, 0), ("y", 1, 2, 1),
+    ("y", 0, 3, 1), ("x", 0, -1, 0, 1), ("y", 0, 3, -1), ("sort", 5), ("flush", 30), ("y", 2, 2, 1),
+    ("x", 1, 1, 1, 1), ("xf", 0, -1, 0), ("y", 2, 2, -1), ("own", 0, 0), ("own", 1, 0), ("y", 3, 3, 1),
+    ("y", 3, 3, -1), ("x", 1, 1, 1, -1), ("x", 1, -1, 1, -1), ("flush", 30), ("y", 1, 3, 1),
+    ("y", 1, 3, -1), ("x", 1, -1, 0, -1), ("y", 0, 4), ("own", 2, 0), ("x", 1, 1, 0, -1), ("xf", 1, 1, 0),
+    ("flush", 30), ("y", 2, 3, 1), ("y", 2, 3, -1), ("xf", 0, 1, 1), ("xf", 0, -1, 1), ("x", 1, -1, 0, 1),
+    ("y", 3, 4), ("own", 3, 0), ("xf", 1, 1, 1), ("y", 1, 4), ("own", 0, 1), ("x", 1, 1, 0, 1),
+    ("xf", 1, -1, 1), ("xf", 1, -1, 0), ("x", 1, -1, 1, 1), ("mirror", 0, 0), ("mirror", 0, 1),
+    ("mirror", 1, 0), ("y", 2, 4), ("mirror", 3, 0), ("own", 3, 1), ("mirror", 3, 1), ("own", 1, 1),
+    ("mirror", 2, 0), ("mirror", 1, 1), ("own", 2, 1), ("mirror", 2, 1),
 )
 
 
@@ -263,8 +266,8 @@
         b = jnp.dot(left(slice(1024, 2048)), right, preferred_element_type=jnp.float32)
         return jnp.where(zero, a, b)
 
-    def on_inverse():
-        @pl.loop(0, 12)
+    def on_inverse(part):
+        @pl.loop(3 * part, 3 * part + 3)
         def _(t):
             inverse[t] = 1.0 / (vir_energy[pl.ds(t, 1), :] - occ_column[...])
 
@@ -296,30 +299,34 @@
 
         return jnp.where(low, tile(2 * b, 0), tile(2 * b + 1, 1)).astype(jnp.bfloat16)
 
-    def on_sort():
-        @pl.loop(0, 16)
+    def on_sort(part):
+        @pl.loop(2 * part, 2 * part + 2)
         def _(b):
             lanes = pl.ds(pl.multiple_of(128 * b, 128), 128)
             own[:, lanes] = sorted_block(lambda i: plain[i].reshape(512, 128), b, 512)
+
+    def on_flush(rest):
+        while len(pending) > rest:
+            pending.pop(0)()
 
     def local(source, target, k):
         copy = pltpu.make_async_copy(source, target, local_sems.at[k])
         copy.start()
         return copy
-
-    labels_copies = [local(row_labels_hbm, row_labels, 0), local(column_labels_hbm, column_labels, 1)]
-    plain_copies = [local(amplitudes.at[:, :, pl.ds(128 * b, 128)], plain.at[b], 8 + b) for b in range(16)]
-    energy_copies = [local(occ_energy_hbm, occ_energy, 3), local(vir_energy_hbm, vir_energy, 4)]
-
-    @pl.when(owner)
-    def _():
-        pltpu.make_async_copy(integrals.at[:, columns_of(zh)], first.at[zh], local_sems.at[6]).start()
 
     barrier = pltpu.get_barrier_semaphore()
     peers = [(at(dy=d), vir) for d in (1, -1, 2, -2, 3, -3, 4)] + [(at(dz=d), vir) for d in (1, -1, 2)]
     peers += [(at(sibling=True), vir), (occ, vir_at(0, True)), (occ, vir_at(1)), (occ, vir_at(-1))]
     for peer in peers:
         pl.semaphore_signal(barrier, inc=1, device_id=peer, device_id_type=MESH)
+
+    labels_copies = [local(row_labels_hbm, row_labels, 0), local(column_labels_hbm, column_labels, 1)]
+    plain_copies = [local(amplitudes.at[:, :, pl.ds(128 * b, 128)], plain.at[b], 8 + b) for b in range(16)]
+    energy_copies = [local(occ_energy_hbm, occ_energy, 3), local(vir_energy_hbm, vir_energy, 4)]
+
+    @pl.when(owner)
+    def _():
+        pltpu.make_async_copy(integrals.at[:, columns_of(zh)], first.at[zh], local_sems.at[6]).start()
 
     pl.semaphore_wait(barrier, len(peers))
     send_first()
@@ -358,12 +365,11 @@
     handlers = {
         "a1": on_first, "a2": on_second, "z": on_z, "y": on_y, "relay": on_relay, "mir": on_mir,
         "zl": on_zl, "x": on_x, "xf": on_xf, "sort": on_sort, "inverse": on_inverse, "own": on_own,
-        "mirror": on_mirror,
+        "mirror": on_mirror, "flush": on_flush,
     }
     for kind, *place in ORDER:
         handlers[kind](*place)
-    for wait in pending:
-        wait()
+    on_flush(0)
 
 
 def body(amplitudes, integrals, row_irreps, column_irreps, occ_energy, vir_energy):

time: 57.6 us -> 57.9 us (level)
  no operation moved by 1% of the time
where the time goes in v6:
time: 57.9 us; the launch traced here: 57.8 us
  Pallas kernels  56.6 us (98%)
  local copies, waits for them, and re-layouts  1.15 us (2%)
    pallas_call x1, Pallas kernels, body(): pl.pallas_call(kernel, out_shape=pltpu.VMEM((512, 1536), jnp.bfloat16), i...  56.6 us

profile of v6, /device:TPU:1, one launch (start us, length us, event | category | flops | bytes accessed | tf_op | source)
XLA Modules:
  0.0 57.8 jit_solution(14071756903980653818)
XLA Ops:
  0.0 56.6 %shard_map.64 = bf16[512,1536]{1,0:T(8,128)(2,1)S(1)} custom-call(s32[32]{0:T(128)} %row_labels_hbm.1, s32[24]{0:T(128)} %column_labels_hbm.1, bf16[32,1536]{1,0:T(8,128)(2,1)} %integrals.1, bf16[8,64,2048]{2,1,0:T(8,128)(2,1)} %bitcast.3, f32[4,128]{1,0:T(4,128)} %bitcast.5, f32[12,128]{1,0:T(8,128)} %bitcast.4), custom_call_target="tpu_custom_call" | custom-call | flops 6442450944 | bytes 4194304 | tf_op jit(solution)/shard_map/pallas_call | solution.py:377
  56.6 1.1 %copy.8 = bf16[512,1536]{1,0:T(8,128)(2,1)} copy(bf16[512,1536]{1,0:T(8,128)(2,1)S(1)} %shard_map.64) | data formatting | bytes 3145728

commit v7 on v6

--- a/solution.py
+++ b/solution.py
@@ -27,14 +27,13 @@
     ("flush", 30), ("y", 2, 3, 1), ("y", 2, 3, -1), ("xf", 0, 1, 1), ("xf", 0, -1, 1), ("x", 1, -1, 0, 1),
     ("y", 3, 4), ("own", 3, 0), ("xf", 1, 1, 1), ("y", 1, 4), ("own", 0, 1), ("x", 1, 1, 0, 1),
     ("xf", 1, -1, 1), ("xf", 1, -1, 0), ("x", 1, -1, 1, 1), ("mirror", 0, 0), ("mirror", 0, 1),
-    ("mirror", 1, 0), ("y", 2, 4), ("mirror", 3, 0), ("own", 3, 1), ("mirror", 3, 1), ("own", 1, 1),
-    ("mirror", 2, 0), ("mirror", 1, 1), ("own", 2, 1), ("mirror", 2, 1),
+    ("mirror", 1, 0), ("y", 2, 4), ("mirror", 3, 0), ("full", 3, 1),     ("mirror", 2, 0), ("full", 1, 1), ("full", 2, 1),
 )
 
 
 def kernel(
     row_labels_hbm, column_labels_hbm, integrals, amplitudes, occ_energy_hbm, vir_energy_hbm, out,
-    packed, mirrored, plain, own, total, inverse, first, second, relay, landed_0, landed_1, landed_2, landed_3, occ_energy, vir_energy, occ_column, zeros,
+    packed, mirrored, plain, eighth, own, total, inverse, first, second, relay, landed_0, landed_1, landed_2, landed_3, occ_energy, vir_energy, occ_column, zeros,
     order_vmem, order, row_labels, column_labels, send_sems, recv_sems, local_sems,
 ):
     landed = (landed_0, landed_1, landed_2, landed_3)
@@ -198,7 +197,7 @@
 
     def send_mirror(way, part):
         rows = pl.ds(16 * index_of(way, part), 16)
-        send(("relay", way, part), lambda: plain.at[:, vir, rows], relay_of(way, part), at(dy=2 * way))
+        send(("relay", way, part), lambda: eighth.at[:, rows], relay_of(way, part), at(dy=2 * way))
 
     def on_relay(way, part):
         arrived(("relay", way, part), relay_of(way, part))
@@ -258,36 +257,55 @@
         block = (zh + stream) % NZ
         return [4 * block + (y // 2 + jnp.where(odd == 1, o, e) + 4) % 4 for e, o in steps]
 
-    def product(tiles, left):
+    def product(tiles, *lefts):
         lanes = [pl.ds(pl.multiple_of(128 * t, 128), 128) for t in tiles]
         right = jnp.concatenate([packed[:, :, :, n].reshape(1024, 128) for n in lanes], axis=1)
         zero = jnp.concatenate([zeros[t] for t in tiles], axis=1) == 1
-        a = jnp.dot(left(slice(0, 1024)), right, preferred_element_type=jnp.float32)
-        b = jnp.dot(left(slice(1024, 2048)), right, preferred_element_type=jnp.float32)
-        return jnp.where(zero, a, b)
+
+        def of_label(part):
+            first, *rest = [jnp.dot(left(part), right, preferred_element_type=jnp.float32) for left in lefts]
+            return first - rest[0] if rest else first
+
+        return jnp.where(zero, of_label(slice(0, 1024)), of_label(slice(1024, 2048)))
+
+    def own_rows(part):
+        return own[:, part]
+
+    def mirrored_rows(part):
+        return mirrored[:, :, :, part].reshape(512, 1024)
+
+    def store(tiles, value):
+        for n, t in enumerate(tiles):
+            columns = pl.ds(pl.multiple_of(128 * t, 128), 128)
+            out[:, columns] = (value[:, 128 * n : 128 * n + 128] * inverse[t]).astype(jnp.bfloat16)
 
     def on_inverse(part):
         @pl.loop(3 * part, 3 * part + 3)
         def _(t):
             inverse[t] = 1.0 / (vir_energy[pl.ds(t, 1), :] - occ_column[...])
 
+    def wait_siblings(stream, half):
+        for delta in needs[half]:
+            arrived(("sib", delta, stream), slot(delta, stream, sibling=True))
+
     def on_own(stream, half):
         @pl.when(valid(stream))
         def _():
-            for delta in needs[half]:
-                arrived(("sib", delta, stream), slot(delta, stream, sibling=True))
-            total[2 * stream + half] = product(tiles_of(stream, half), lambda lanes: own[:, lanes])
+            wait_siblings(stream, half)
+            total[2 * stream + half] = product(tiles_of(stream, half), own_rows)
 
     def on_mirror(stream, half):
         @pl.when(valid(stream))
         def _():
             tiles = tiles_of(stream, half)
-            value = total[2 * stream + half] - product(
-                tiles, lambda lanes: mirrored[:, :, :, lanes].reshape(512, 1024)
-            )
-            for n, t in enumerate(tiles):
-                columns = pl.ds(pl.multiple_of(128 * t, 128), 128)
-                out[:, columns] = (value[:, 128 * n : 128 * n + 128] * inverse[t]).astype(jnp.bfloat16)
+            store(tiles, total[2 * stream + half] - product(tiles, mirrored_rows))
+
+    def on_full(stream, half):
+        @pl.when(valid(stream))
+        def _():
+            wait_siblings(stream, half)
+            tiles = tiles_of(stream, half)
+            store(tiles, product(tiles, own_rows, mirrored_rows))
 
     def sorted_block(block, b, rows):
         low = lax.broadcasted_iota(jnp.int32, (rows, 128), 1) < TILE
@@ -320,8 +338,8 @@
     for peer in peers:
         pl.semaphore_signal(barrier, inc=1, device_id=peer, device_id_type=MESH)
 
+    eighth_copies = [local(amplitudes.at[vir, :, pl.ds(128 * b, 128)], eighth.at[b], 24 + b) for b in range(16)]
     labels_copies = [local(row_labels_hbm, row_labels, 0), local(column_labels_hbm, column_labels, 1)]
-    plain_copies = [local(amplitudes.at[:, :, pl.ds(128 * b, 128)], plain.at[b], 8 + b) for b in range(16)]
     energy_copies = [local(occ_energy_hbm, occ_energy, 3), local(vir_energy_hbm, vir_energy, 4)]
 
     @pl.when(owner)
@@ -330,11 +348,12 @@
 
     pl.semaphore_wait(barrier, len(peers))
     send_first()
-    for copy in plain_copies:
+    for copy in eighth_copies:
         copy.wait()
     for part in (0, 1):
         for way in (1, -1):
             send_mirror(way, part)
+    plain_copies = [local(amplitudes.at[:, :, pl.ds(128 * b, 128)], plain.at[b], 8 + b) for b in range(16)]
 
     for copy in labels_copies:
         copy.wait()
@@ -361,11 +380,13 @@
             jnp.broadcast_to(occ_energy[b : b + 1, :], (128, 128))
         )
     order_copy.wait()
+    for copy in plain_copies:
+        copy.wait()
 
     handlers = {
         "a1": on_first, "a2": on_second, "z": on_z, "y": on_y, "relay": on_relay, "mir": on_mir,
         "zl": on_zl, "x": on_x, "xf": on_xf, "sort": on_sort, "inverse": on_inverse, "own": on_own,
-        "mirror": on_mirror, "flush": on_flush,
+        "mirror": on_mirror, "full": on_full, "flush": on_flush,
     }
     for kind, *place in ORDER:
         handlers[kind](*place)
@@ -383,6 +404,7 @@
             pltpu.VMEM((16, 4, 16, 1536), jnp.bfloat16),
             pltpu.VMEM((8, 4, 16, 2048), jnp.bfloat16),
             pltpu.VMEM((16, 8, 64, 128), jnp.bfloat16),
+            pltpu.VMEM((16, 64, 128), jnp.bfloat16),
             pltpu.VMEM((512, 2048), jnp.bfloat16),
             pltpu.VMEM((8, 512, 256), jnp.float32),
             pltpu.VMEM((12, 512, 128), jnp.float32),
@@ -400,7 +422,7 @@
             pltpu.SMEM((24,), jnp.int32),
             pltpu.SemaphoreType.DMA((N_SEMS,)),
             pltpu.SemaphoreType.DMA((N_SEMS,)),
-            pltpu.SemaphoreType.DMA((24,)),
+            pltpu.SemaphoreType.DMA((40,)),
         ],
         compiler_params=pltpu.CompilerParams(
             collective_id=0, has_side_effects=True, vmem_limit_bytes=58 * 2**20

time: 57.9 us -> 58.1 us (level)
  no operation moved by 1% of the time
where the time goes in v7:
time: 58.1 us; the launch traced here: 57.9 us
  Pallas kernels  56.8 us (98%)
  local copies, waits for them, and re-layouts  1.15 us (2%)
    pallas_call x1, Pallas kernels, body(): pl.pallas_call(kernel, out_shape=pltpu.VMEM((512, 1536), jnp.bfloat16), i...  56.8 us

profile of v7, /device:TPU:1, one launch (start us, length us, event | category | flops | bytes accessed | tf_op | source)
XLA Modules:
  0.0 57.9 jit_solution(5804376714073722543)
XLA Ops:
  0.0 56.8 %shard_map.64 = bf16[512,1536]{1,0:T(8,128)(2,1)S(1)} custom-call(s32[32]{0:T(128)} %row_labels_hbm.1, s32[24]{0:T(128)} %column_labels_hbm.1, bf16[32,1536]{1,0:T(8,128)(2,1)} %integrals.1, bf16[8,64,2048]{2,1,0:T(8,128)(2,1)} %bitcast.3, f32[4,128]{1,0:T(4,128)} %bitcast.5, f32[12,128]{1,0:T(8,128)} %bitcast.4), custom_call_target="tpu_custom_call" | custom-call | flops 6442450944 | bytes 4194304 | tf_op jit(solution)/shard_map/pallas_call | solution.py:398
  56.8 1.1 %copy.8 = bf16[512,1536]{1,0:T(8,128)(2,1)} copy(bf16[512,1536]{1,0:T(8,128)(2,1)S(1)} %shard_map.64) | data formatting | bytes 3145728
